TPU v7x, 128 devices: a whole 4x4x4 slice. The times are simulated.
128 devices in a mesh: row: 8 (over x, core), col: 16 (over z, y).
Axes of the slice: x: 4, y: 4, z: 4, core: 2. Of those that a mesh axis runs over, the one named last changes fastest.
Arguments:
- force: float32 [3, 128, 256, 512], P(None, 'row', 'col'), may hold values from -8 to 8
- multiplier: float32 [6, 128, 256, 512], P(None, 'row', 'col'), may hold values from -6 to 6
- strain_aux: float32 [6, 128, 256, 512], P(None, 'row', 'col'), may hold values from -4 to 4
- entry_lines: int32 [16384], P(('row', 'col')), may hold values from 0 to 1023, as said below
- entry_owner: int32 [16384, 1], P(('row', 'col')), may hold values from 0 to 127, as said below
- entry_slot: int32 [16384], P(('row', 'col')), may hold values from 0 to 71
Outputs:
- velocity: float32 [3, 128, 256, 512], P(None, 'row', 'col')
- new_aux: float32 [6, 128, 256, 512], P(None, 'row', 'col')
- new_multiplier: float32 [6, 128, 256, 512], P(None, 'row', 'col')
Inputs may be any that keep to these rules, and one draw needn't show every extreme that they name: `entry_owner`: margins come in runs of four consecutive entries naming one owner and one slot. Among the margins listed on one device, no owner is named more than 4 times (one run), and the listing device itself exactly 4 times. `entry_lines`: each run of four consecutive margins covers a 2 x 2 patch of neighbouring lines in y and z with the same x block.
All inputs are finite; a program needn't handle non-finite values.
Results may differ from a plain program's by a relative error of at most 0.0003.
Values sent between devices are 32-bit elements; how exact they have to be, the bound alone decides.
A program may use at most 192 MiB of HBM per device.

v0:
```python
import math

import jax
import jax.numpy as jnp
from jax import lax
from jax.sharding import PartitionSpec as P

BL = 128
NPD = 72


mass_coef = 0.02
visc_coef = 10.0
penalty = 5.0
yield_stress = 2.0
highest = lax.Precision.HIGHEST


def extended(cells, sides, width):
    for axis, dim in sides:
        count = lax.axis_size(axis)
        head = lax.slice_in_dim(cells, 0, width, axis=dim)
        tail = lax.slice_in_dim(cells, cells.shape[dim] - width, cells.shape[dim], axis=dim)
        cells = jnp.concatenate(
            [
                lax.ppermute(tail, axis, [(i, (i + 1) % count) for i in range(count)]),
                cells,
                lax.ppermute(head, axis, [((i + 1) % count, i) for i in range(count)]),
            ],
            axis=dim,
        )
    return cells


def centered(lower2, lower1, upper1, upper2):
    return (8.0 * (upper1 - lower1) - (upper2 - lower2)) / 12.0


def along_x(field):
    return centered(
        jnp.roll(field, 2, -1),
        jnp.roll(field, 1, -1),
        jnp.roll(field, -1, -1),
        jnp.roll(field, -2, -1),
    )


def along_y(padded):
    return centered(padded[:, 0:-4], padded[:, 1:-3], padded[:, 3:-1], padded[:, 4:])


def along_z(padded):
    return centered(padded[:, :, 0:-4], padded[:, :, 1:-3], padded[:, :, 3:-1], padded[:, :, 4:])


def tables(rows, cols, total):
    left = jnp.arange(rows, dtype=jnp.int32)[:, None]
    right = jnp.arange(cols, dtype=jnp.int32)[None, :]
    angle = (left * right % total).astype(jnp.float32) * (2.0 * math.pi / total)
    return (jnp.cos(angle), jnp.sin(angle))


def wave_numbers(start, count, total):
    marks = start + jnp.arange(count, dtype=jnp.int32)
    signed = jnp.where(marks < total // 2, marks, marks - total)
    waves = signed.astype(jnp.float32) * (2.0 * math.pi / total)
    keeper = (marks != total // 2).astype(jnp.float32)
    return (waves, keeper)


def forward_pair(real_part, imag_part, form, cosines, sines):
    real_out = jnp.einsum(form, real_part, cosines, precision=highest) + jnp.einsum(
        form, imag_part, sines, precision=highest
    )
    imag_out = jnp.einsum(form, imag_part, cosines, precision=highest) - jnp.einsum(
        form, real_part, sines, precision=highest
    )
    return jnp.stack([real_out, imag_out])


def inverse_pair(real_part, imag_part, form, cosines, sines):
    real_out = jnp.einsum(form, real_part, cosines, precision=highest) - jnp.einsum(
        form, imag_part, sines, precision=highest
    )
    imag_out = jnp.einsum(form, real_part, sines, precision=highest) + jnp.einsum(
        form, imag_part, cosines, precision=highest
    )
    return jnp.stack([real_out, imag_out])


def stokes(rhs):
    comps, cells_y, cells_z, cells_x = rhs.shape
    total_y = cells_y * lax.axis_size("row")
    total_z = cells_z * lax.axis_size("col")
    cos_x, sin_x = tables(cells_x, cells_x, cells_x)
    spec = jnp.stack(
        [
            jnp.einsum("cyzx,xm->cmzy", rhs, cos_x, precision=highest),
            -jnp.einsum("cyzx,xm->cmzy", rhs, sin_x, precision=highest),
        ]
    )
    spec = lax.all_to_all(spec, "row", split_axis=2, concat_axis=4, tiled=True)
    cos_y, sin_y = tables(total_y, total_y, total_y)
    spec = forward_pair(spec[0], spec[1], "cmzy,yk->cmkz", cos_y, sin_y)
    spec = lax.all_to_all(spec, "col", split_axis=3, concat_axis=4, tiled=True)
    cos_z, sin_z = tables(total_z, total_z, total_z)
    spec = forward_pair(spec[0], spec[1], "cmkz,zl->cmkl", cos_z, sin_z)
    part_x = spec.shape[2]
    part_y = spec.shape[3]
    wave_x, keep_x = wave_numbers(lax.axis_index("row") * part_x, part_x, cells_x)
    wave_y, keep_y = wave_numbers(lax.axis_index("col") * part_y, part_y, total_y)
    wave_z, keep_z = wave_numbers(jnp.int32(0), total_z, total_z)
    wave_x, keep_x = (wave_x.reshape(part_x, 1, 1), keep_x.reshape(part_x, 1, 1))
    wave_y, keep_y = (wave_y.reshape(1, part_y, 1), keep_y.reshape(1, part_y, 1))
    wave_z, keep_z = (wave_z.reshape(1, 1, total_z), keep_z.reshape(1, 1, total_z))
    dotk = wave_x * spec[:, 0] + wave_y * spec[:, 1] + wave_z * spec[:, 2]
    ksq = wave_x * wave_x + wave_y * wave_y + wave_z * wave_z
    ksafe = jnp.where(ksq > 0, ksq, 1.0)
    gain = keep_x * keep_y * keep_z / (mass_coef + visc_coef * ksq)
    spec = jnp.stack(
        [
            (spec[:, 0] - wave_x * dotk / ksafe) * gain,
            (spec[:, 1] - wave_y * dotk / ksafe) * gain,
            (spec[:, 2] - wave_z * dotk / ksafe) * gain,
        ],
        axis=1,
    )
    spec = inverse_pair(spec[0], spec[1], "cmkl,lz->cmkz", cos_z, sin_z)
    spec = lax.all_to_all(spec, "col", split_axis=4, concat_axis=3, tiled=True)
    spec = inverse_pair(spec[0], spec[1], "cmkz,ky->cmzy", cos_y, sin_y)
    spec = lax.all_to_all(spec, "row", split_axis=4, concat_axis=2, tiled=True)
    back_cos, back_sin = tables(cells_x, cells_x, cells_x)
    weights = jnp.ones((cells_x,), jnp.float32)
    weights = (weights / float(cells_x * total_y * total_z))[:, None]
    return jnp.einsum("cmzy,mx->cyzx", spec[0], back_cos * weights, precision=highest) - jnp.einsum(
        "cmzy,mx->cyzx", spec[1], back_sin * weights, precision=highest
    )


def cross_terms(first, second):
    return (
        first[1] * second[2] - first[2] * second[1],
        first[2] * second[0] - first[0] * second[2],
        first[0] * second[1] - first[1] * second[0],
    )


def collect(values, hot):
    return jnp.dot(values, hot, precision=highest)


def spread_back(params, hot):
    return jnp.dot(params, hot.T, precision=highest)


def owner_blocks(recv_vel, recv_meta):
    slot_ids = recv_meta[0]
    valid = (slot_ids >= 0).astype(jnp.float32)
    hot = (slot_ids[:, None] == jnp.arange(NPD, dtype=jnp.int32)[None, :]).astype(jnp.float32)
    pos_y = recv_meta[1].astype(jnp.float32)
    pos_z = recv_meta[2].astype(jnp.float32)
    pos_x = recv_meta[3].astype(jnp.float32)
    offsets = jnp.arange(BL, dtype=jnp.float32)[None, :]
    sums = jnp.stack(
        [
            valid * BL,
            valid * (BL * pos_x + BL * (BL - 1) / 2.0),
            valid * BL * pos_y,
            valid * BL * pos_z,
        ]
    )
    totals = collect(sums, hot)
    safe_n = jnp.maximum(totals[0], 1.0)
    centers = spread_back(totals[1:4] / safe_n, hot)
    rel_x = (pos_x[:, None] + offsets - centers[0][:, None]) * valid[:, None]
    rel_y = (pos_y - centers[1])[:, None] * valid[:, None] + jnp.zeros((1, BL), jnp.float32)
    rel_z = (pos_z - centers[2])[:, None] * valid[:, None] + jnp.zeros((1, BL), jnp.float32)
    vel_x, vel_y, vel_z = (recv_vel[0], recv_vel[1], recv_vel[2])
    moment = jnp.stack(
        [
            jnp.sum(vel_x, axis=1),
            jnp.sum(vel_y, axis=1),
            jnp.sum(vel_z, axis=1),
            jnp.sum(rel_y * vel_z - rel_z * vel_y, axis=1),
            jnp.sum(rel_z * vel_x - rel_x * vel_z, axis=1),
            jnp.sum(rel_x * vel_y - rel_y * vel_x, axis=1),
            jnp.sum(rel_x * rel_x + rel_y * rel_y + rel_z * rel_z, axis=1),
        ]
    )
    gathered = collect(moment, hot)
    inertia = jnp.maximum(gathered[6] * (2.0 / 3.0), 1.0)
    params = jnp.concatenate([gathered[0:3] / safe_n, gathered[3:6] / inertia], axis=0)
    fitted = spread_back(params, hot)
    spin = (fitted[3][:, None], fitted[4][:, None], fitted[5][:, None])
    turn = cross_terms(spin, (rel_x, rel_y, rel_z))
    rigid = jnp.stack(
        [fitted[0][:, None] + turn[0], fitted[1][:, None] + turn[1], fitted[2][:, None] + turn[2]]
    )
    return (rigid - recv_vel) * valid[None, :, None]


def project(fluid, entry_lines, entry_owner, entry_slot):
    comps, cells_y, cells_z, cells_x = fluid.shape
    per_line = cells_x // BL
    lines_all = fluid.reshape(comps, cells_y * cells_z * per_line, BL)
    count = entry_lines.shape[0]
    devices = lax.axis_size("row") * lax.axis_size("col")
    capacity = 4
    line_y = entry_lines // (cells_z * per_line)
    line_z = entry_lines // per_line % cells_z
    glob_y = lax.axis_index("row") * cells_y + line_y
    glob_z = lax.axis_index("col") * cells_z + line_z
    glob_x = entry_lines % per_line * BL
    blocks = jnp.take(lines_all, entry_lines, axis=1)
    target = entry_owner[:, 0]
    hits = (target[:, None] == jnp.arange(devices, dtype=jnp.int32)[None, :]).astype(jnp.int32)
    before = jnp.cumsum(hits, axis=0) - hits
    rank = jnp.sum(before * hits, axis=1)
    placed = target * capacity + rank
    slot_entry = (
        jnp.full((devices * capacity,), -1, jnp.int32)
        .at[placed]
        .set(jnp.arange(count, dtype=jnp.int32))
    )
    filled = slot_entry >= 0
    source = jnp.maximum(slot_entry, 0)
    slot_meta = jnp.where(filled, entry_slot[source], -1)
    send_vel = jnp.take(blocks, source, axis=1) * filled.astype(jnp.float32)[None, :, None]
    meta = jnp.stack([slot_meta, glob_y[source], glob_z[source], glob_x[source]])
    recv_vel, recv_meta = (
        lax.all_to_all(send_vel, ("row", "col"), split_axis=1, concat_axis=1, tiled=True),
        lax.all_to_all(meta, ("row", "col"), split_axis=1, concat_axis=1, tiled=True),
    )
    fixes = owner_blocks(recv_vel, recv_meta)
    returned = lax.all_to_all(fixes, ("row", "col"), split_axis=1, concat_axis=1, tiled=True)
    correction = jnp.take(returned, placed, axis=1)
    lines_all = lines_all.at[:, entry_lines, :].add(correction)
    return lines_all.reshape(fluid.shape)


def local(force, multiplier, strain_aux, entry_lines, entry_owner, entry_slot):
    shifted = multiplier - penalty * strain_aux
    rim_part = extended(shifted[1:6], (("row", 1), ("col", 2)), 2)
    rims_y = rim_part[:, :, 2:-2, :]
    rims_z = rim_part[:, 2:-2, :, :]
    deriv_y = along_y(rims_y)
    deriv_z = along_z(rims_z)
    rhs_x = force[0] + along_x(shifted[0]) + deriv_y[2] + deriv_z[3]
    rhs_y = force[1] + along_x(shifted[3]) + deriv_y[0] + deriv_z[4]
    rhs_z = force[2] + along_x(shifted[4]) + deriv_y[4] + deriv_z[1]
    fluid = stokes(jnp.stack([rhs_x, rhs_y, rhs_z]))
    velocity = project(fluid, entry_lines, entry_owner, entry_slot)
    padded = extended(velocity, (("row", 1), ("col", 2)), 2)
    vel_dy = along_y(padded[:, :, 2:-2, :])
    vel_dz = along_z(padded[:, 2:-2, :, :])
    vel_dx = along_x(velocity)
    strain = jnp.stack(
        [
            vel_dx[0],
            vel_dy[1],
            vel_dz[2],
            (vel_dy[0] + vel_dx[1]) / 2.0,
            (vel_dz[0] + vel_dx[2]) / 2.0,
            (vel_dz[1] + vel_dy[2]) / 2.0,
        ]
    )
    q_field = multiplier + penalty * strain
    qnorm = jnp.sqrt(
        q_field[0] ** 2
        + q_field[1] ** 2
        + q_field[2] ** 2
        + 2.0 * (q_field[3] ** 2 + q_field[4] ** 2 + q_field[5] ** 2)
    )
    factor = 1.0 - yield_stress / jnp.maximum(qnorm, yield_stress)
    new_aux = factor[None] * q_field / penalty
    new_multiplier = multiplier + penalty * (strain - new_aux)
    return (velocity, new_aux, new_multiplier)


def solution(mesh):
    in_specs = (
        P(None, "row", "col", None),
        P(None, "row", "col", None),
        P(None, "row", "col", None),
        P(("row", "col")),
        P(("row", "col"), None),
        P(("row", "col")),
    )
    out_specs = (
        P(None, "row", "col", None),
        P(None, "row", "col", None),
        P(None, "row", "col", None),
    )
    return jax.shard_map(local, mesh=mesh, in_specs=in_specs, out_specs=out_specs, check_vma=False)
```

profile of v0, /device:TPU:1, one launch (start us, length us, event | category | flops | bytes accessed | tf_op | source)
XLA Modules:
  0.0 647.6 jit_solution(13117781101785008329)
XLA Ops:
  35.4 6.5 convolution_bitcast_fusion
  41.9 7.0 %negate_bitcast_fusion = f32[1,3,512,16,16]{2,3,4,1,0:T(8,128)S(1)} fusion(f32[1,16,16,512]{3,2,1,0:T(8,128)S(1)} %slice_add_fusion.3, f32[1,16,16,512]{3,2,1,0:T(8,128)S(1)} %slice_add_fusion.5, f32[1,16,16,512]{3,2,1,0:T(8,128)S(1)} %slice_add_fusion.7), kind=kOutput, calls=%fused_computation.77 | convolution fusion | flops 2420768768 | bytes 3145728 | tf_op jit(solution)/shard_map/cyzx,xm->cmzy/dot_general | solution.py:99
  49.2 19.9 %copy.262 = f32[2,3,512,16,16]{3,4,1,0,2:T(8,128)} copy(f32[2,3,512,16,16]{2,3,4,1,0:T(8,128)S(1)} %pad_maximum_fusion.1) | data formatting | bytes 6291456 | tf_op jit(solution)/shard_map/stack | solution.py:96
  69.1 13.7 %reshape.1144 = f32[8,1,98304]{2,1,0:T(1,128)S(1)} reshape(f32[512,2,3,16,16]{4,3,2,1,0:T(8,128)} %bitcast.262) | data formatting | bytes 6291456
  82.8 47.8 %all_to_all.76 = f32[8,1,98304]{2,1,0:T(1,128)} all-to-all(f32[8,1,98304]{2,1,0:T(1,128)S(1)} %reshape.1144), channel_id=1, replica_groups=mesh['row'=8,'col'=16] {'row'}, dimensions={0} | all-to-all | bytes 6291456 | tf_op jit(solution)/shard_map/all_to_all | solution.py:102
  131.1 10.3 %reduce.31 = f32[8,98304]{1,0:T(8,128)S(1)} reduce(f32[8,1,98304]{2,1,0:T(1,128)} %all_to_all.76, f32[]{:T(128)} %broadcast.1011), dimensions={1}, to_apply=%all_to_all.54.reduce_sub_computation | reduce | bytes 6291460 | tf_op jit(solution)/shard_map/all_to_all | solution.py:102
  141.4 17.0 %reshape.1145 = f32[512,2,3,16,16]{4,3,2,1,0:T(8,128)} reshape(f32[8,98304]{1,0:T(8,128)S(1)} %reduce.31) | data formatting | bytes 6291456
  158.4 18.9 %copy.263 = f32[2,3,8,64,16,16]{3,5,2,4,1,0:T(8,128)} copy(f32[2,3,8,64,16,16]{4,5,1,0,3,2:T(8,128)} %bitcast.263) | data formatting | bytes 6291456 | tf_op jit(solution)/shard_map/all_to_all | solution.py:102
  208.1 8.5 %reshape.1146 = f32[16,1,49152]{2,1,0:T(1,128)} reshape(f32[128,2,3,16,64]{4,3,2,1,0:T(8,128)} %bitcast.271) | data formatting | bytes 6291456
  222.1 45.0 %all-to-all-done.1 = f32[16,1,49152]{2,1,0:T(1,128)S(1)} async-done(((f32[16,1,49152]{2,1,0:T(1,128)}), f32[16,1,49152]{2,1,0:T(1,128)S(1)}, u32[]{:S(2)}, u32[]{:S(2)}) %all-to-all-start.1) | async-done | bytes 3145760 | tf_op jit(solution)/shard_map/all_to_all | solution.py:105
  267.1 11.1 %reduce.32 = f32[16,49152]{1,0:T(8,128)} reduce(f32[16,1,49152]{2,1,0:T(1,128)S(1)} %all-to-all-done.1, f32[]{:T(128)} %broadcast.1011), dimensions={1}, to_apply=%all_to_all.57.reduce_sub_computation | reduce | bytes 6291460 | tf_op jit(solution)/shard_map/all_to_all | solution.py:105
  326.5 8.5 %reshape.1148 = f32[16,1,49152]{2,1,0:T(1,128)} reshape(f32[256,2,3,8,64]{4,3,2,1,0:T(8,128)} %bitcast.273) | data formatting | bytes 6291456
  357.1 24.5 %all-to-all-done.2 = f32[16,1,49152]{2,1,0:T(1,128)S(1)} async-done(((f32[16,1,49152]{2,1,0:T(1,128)}), f32[16,1,49152]{2,1,0:T(1,128)S(1)}, u32[]{:S(2)}, u32[]{:S(2)}) %all-to-all-start.2) | async-done | bytes 3145760 | tf_op jit(solution)/shard_map/all_to_all | solution.py:129
  381.6 9.6 %all-to-all-start.5 = ((s32[4,128,4]{2,0,1:T(4,128)}), s32[4,128,4]{2,0,1:T(4,128)S(1)}, u32[]{:S(2)}, u32[]{:S(2)}) async-start(s32[4,128,4]{2,0,1:T(4,128)} %copy.292), calls=%async_computation.5 | async-start | bytes 524288 | tf_op jit(solution)/shard_map/all_to_all | solution.py:232
  391.2 10.9 %reduce.33 = f32[16,49152]{1,0:T(8,128)} reduce(f32[16,1,49152]{2,1,0:T(1,128)S(1)} %all-to-all-done.2, f32[]{:T(128)} %broadcast.1011), dimensions={1}, to_apply=%all_to_all.60.reduce_sub_computation | reduce | bytes 6291460 | tf_op jit(solution)/shard_map/all_to_all | solution.py:129
  439.9 8.5 %reshape.1150 = f32[8,1,98304]{2,1,0:T(1,128)} reshape(f32[128,2,3,16,64]{4,3,2,1,0:T(8,128)} %bitcast.275) | data formatting | bytes 6291456
  463.4 27.3 %all-to-all-done.3 = f32[8,1,98304]{2,1,0:T(1,128)S(1)} async-done(((f32[8,1,98304]{2,1,0:T(1,128)}), f32[8,1,98304]{2,1,0:T(1,128)S(1)}, u32[]{:S(2)}, u32[]{:S(2)}) %all-to-all-start.3) | async-done | bytes 3145760 | tf_op jit(solution)/shard_map/all_to_all | solution.py:131
  490.8 11.3 %reduce.34 = f32[8,98304]{1,0:T(8,128)} reduce(f32[8,1,98304]{2,1,0:T(1,128)S(1)} %all-to-all-done.3, f32[]{:T(128)} %broadcast.1011), dimensions={1}, to_apply=%all_to_all.63.reduce_sub_computation | reduce | bytes 6291460 | tf_op jit(solution)/shard_map/all_to_all | solution.py:131
  502.1 7.2 %reshape.1151 = f32[128,2,3,16,64]{4,3,2,1,0:T(8,128)} reshape(f32[8,98304]{1,0:T(8,128)} %reduce.34) | data formatting | bytes 6291456
  521.2 9.2 %fusion.34 = f32[512,768]{0,1} fusion(f32[512,768]{0,1:T(8,128)} %bitcast.284), kind=kOutput, calls=%fused_computation.100 | convolution fusion | flops 2419851264 | bytes 3145728
  533.5 8.8 %fusion.32 = f32[512,768]{0,1:S(1)} fusion(f32[512,768]{0,1:T(8,128)} %bitcast.285), kind=kOutput, calls=%fused_computation.94 | convolution fusion | flops 2419851264 | bytes 3145728
  555.7 8.8 %all-to-all-start.4 = ((f32[3,512,128]{2,0,1:T(4,128)}), f32[3,512,128]{2,0,1:T(4,128)S(1)}, u32[]{:S(2)}, u32[]{:S(2)}) async-start(f32[3,512,128]{2,0,1:T(4,128)} %multiply_bitcast_fusion), calls=%async_computation.4 | async-start | bytes 2097152 | tf_op jit(solution)/shard_map/all_to_all | solution.py:231
  565.2 18.0 %all-to-all-done.4 = f32[3,512,128]{2,0,1:T(4,128)S(1)} async-done(((f32[3,512,128]{2,0,1:T(4,128)}), f32[3,512,128]{2,0,1:T(4,128)S(1)}, u32[]{:S(2)}, u32[]{:S(2)}) %all-to-all-start.4) | async-done | bytes 786464 | tf_op jit(solution)/shard_map/all_to_all | solution.py:231
  593.6 18.9 %all-to-all-done.6 = f32[3,512,128]{2,0,1:T(4,128)S(1)} async-done(((f32[3,512,128]{2,0,1:T(4,128)}), f32[3,512,128]{2,0,1:T(4,128)S(1)}, u32[]{:S(2)}, u32[]{:S(2)}) %all-to-all-start.6) | async-done | bytes 786464 | tf_op jit(solution)/shard_map/all_to_all | solution.py:235
  (239 shorter events, 268.8 us)
Async XLA Ops:
  0.6 341.6 %copy-start = (s32[128]{0:T(128)S(1)}, s32[128]{0:T(128)}, u32[]{:S(2)}) copy-start(s32[128]{0:T(128)} %param.11) | copy-start | bytes 1540
  4.7 7.7 %collective-permute-start = (f32[5,2,16,512]{3,2,1,0:T(8,128)S(1)}, f32[5,2,16,512]{3,2,1,0:T(8,128)S(1)}, u32[]{:S(2)}, u32[]{:S(2)}) collective-permute-start(f32[5,2,16,512]{3,2,1,0:T(8,128)S(1)} %get-tuple-element.45), channel_id=1, source_target_pairs={{16,0},{32,16},{48,32},{64,48},{80,64},{96,80},{112,96},{0,112},{1... | collective-permute-start | bytes 983048 | tf_op jit(solution)/shard_map/ppermute | solution.py:28
  6.1 6.2 collective-permute-start.1
  12.7 11.2 %collective-permute-start.2 = (f32[5,20,2,512]{3,2,1,0:T(2,128)S(1)}, f32[5,20,2,512]{3,2,1,0:T(2,128)S(1)}, u32[]{:S(2)}, u32[]{:S(2)}) collective-permute-start(f32[5,20,2,512]{3,2,1,0:T(2,128)S(1)} %get-tuple-element.39), channel_id=1, source_target_pairs={{1,0},{2,1},{3,2},{4,3},{5,4},{6,5},{7,6},{8,7},{9,8},{10,9},{11,1... | collective-permute-start | bytes 1228808 | tf_op jit(solution)/shard_map/ppermute | solution.py:28
  19.0 10.1 %collective-permute-start.3 = (f32[5,20,2,512]{3,2,1,0:T(2,128)S(1)}, f32[5,20,2,512]{3,2,1,0:T(2,128)S(1)}, u32[]{:S(2)}, u32[]{:S(2)}) collective-permute-start(f32[5,20,2,512]{3,2,1,0:T(2,128)S(1)} %get-tuple-element.40), channel_id=1, source_target_pairs={{0,1},{1,2},{2,3},{3,4},{4,5},{5,6},{6,7},{7,8},{8,9},{9,10},{10,1... | collective-permute-start | bytes 1228808 | tf_op jit(solution)/shard_map/ppermute | solution.py:26
  216.5 50.5 %all-to-all-start.1 = ((f32[16,1,49152]{2,1,0:T(1,128)}), f32[16,1,49152]{2,1,0:T(1,128)S(1)}, u32[]{:S(2)}, u32[]{:S(2)}) async-start(f32[16,1,49152]{2,1,0:T(1,128)} %reshape.1146), calls=%async_computation.1 | async-start | bytes 6291456 | tf_op jit(solution)/shard_map/all_to_all | solution.py:105
  335.0 6.6 %copy-start.24 = (s32[128]{0:T(128)S(1)}, s32[128]{0:T(128)}, u32[]{:S(2)}) copy-start(s32[128]{0:T(128)} %param.9) | copy-start | bytes 1540
  335.0 46.6 %all-to-all-start.2 = ((f32[16,1,49152]{2,1,0:T(1,128)}), f32[16,1,49152]{2,1,0:T(1,128)S(1)}, u32[]{:S(2)}, u32[]{:S(2)}) async-start(f32[16,1,49152]{2,1,0:T(1,128)} %reshape.1148), calls=%async_computation.2 | async-start | bytes 6291456 | tf_op jit(solution)/shard_map/all_to_all | solution.py:129
  341.6 7.5 %copy-start.17 = (s32[128]{0:T(128)}, s32[128]{0:T(128)S(1)}, u32[]{:S(2)}) copy-start(s32[128]{0:T(128)S(1)} %get-tuple-element.115) | copy-start | bytes 1540
  342.2 10.4 %copy-start.13 = (s32[1024]{0:T(1024)}, s32[1024]{0:T(1024)S(1)}, u32[]{:S(2)}) copy-start(s32[1024]{0:T(1024)S(1)} %get-tuple-element.130) | copy-start | bytes 12292
  381.6 66.8 %all-to-all-start.5 = ((s32[4,128,4]{2,0,1:T(4,128)}), s32[4,128,4]{2,0,1:T(4,128)S(1)}, u32[]{:S(2)}, u32[]{:S(2)}) async-start(s32[4,128,4]{2,0,1:T(4,128)} %copy.292), calls=%async_computation.5 | async-start | bytes 524288 | tf_op jit(solution)/shard_map/all_to_all | solution.py:232
  448.4 42.4 %all-to-all-start.3 = ((f32[8,1,98304]{2,1,0:T(1,128)}), f32[8,1,98304]{2,1,0:T(1,128)S(1)}, u32[]{:S(2)}, u32[]{:S(2)}) async-start(f32[8,1,98304]{2,1,0:T(1,128)} %reshape.1150), calls=%async_computation.3 | async-start | bytes 6291456 | tf_op jit(solution)/shard_map/all_to_all | solution.py:131
  521.2 9.2 %copy-start.5 = (f32[1,3,8,64,16,16]{3,5,2,4,1,0:T(8,128)S(1)}, f32[1,3,8,64,16,16]{3,5,2,4,1,0:T(8,128)}, u32[]{:S(2)}) copy-start(f32[1,3,8,64,16,16]{3,5,2,4,1,0:T(8,128)} %get-tuple-element.27) | copy-start | bytes 4718596
  533.5 8.9 %copy-start.11 = (f32[512,768]{0,1:S(1)}, f32[512,768]{0,1}, u32[]{:S(2)}) copy-start(f32[512,768]{0,1} %fusion.34) | copy-start | bytes 4718596
  551.2 13.7 %copy-start.12 = (f32[1,128,4]{2,0,1:T(1,128)S(1)}, f32[1,128,4]{2,0,1:T(1,128)}, u32[]{:S(2)}) copy-start(f32[1,128,4]{2,0,1:T(1,128)} %get-tuple-element.87) | copy-start | bytes 6148
  555.7 27.5 %all-to-all-start.4 = ((f32[3,512,128]{2,0,1:T(4,128)}), f32[3,512,128]{2,0,1:T(4,128)S(1)}, u32[]{:S(2)}, u32[]{:S(2)}) async-start(f32[3,512,128]{2,0,1:T(4,128)} %multiply_bitcast_fusion), calls=%async_computation.4 | async-start | bytes 2097152 | tf_op jit(solution)/shard_map/all_to_all | solution.py:231
  587.1 6.4 copy-start.21
  587.2 26.1 %copy-start.19 = (pred[128]{0:T(512)(128)(4,1)S(1)}, pred[128]{0:T(512)(128)(4,1)}, u32[]{:S(2)}) copy-start(pred[128]{0:T(512)(128)(4,1)} %get-tuple-element.16) | copy-start | bytes 388
  588.7 24.8 %copy-start.18 = (s32[128]{0:T(128)S(1)}, s32[128]{0:T(128)}, u32[]{:S(2)}) copy-start(s32[128]{0:T(128)} %copy-done.17) | copy-start | bytes 1540
  588.7 23.8 %all-to-all-start.6 = ((f32[3,512,128]{2,0,1:T(4,128)}), f32[3,512,128]{2,0,1:T(4,128)S(1)}, u32[]{:S(2)}, u32[]{:S(2)}) async-start(f32[3,512,128]{2,0,1:T(4,128)} %copy.294), calls=%async_computation.6 | async-start | bytes 2097152 | tf_op jit(solution)/shard_map/all_to_all | solution.py:235
  622.7 4.2 collective-permute-start.5
  624.3 5.4 collective-permute-start.4
  630.0 6.2 collective-permute-start.6
  630.5 8.5 %collective-permute-start.7 = (f32[3,20,2,512]{3,2,1,0:T(2,128)S(1)}, f32[3,20,2,512]{3,2,1,0:T(2,128)S(1)}, u32[]{:S(2)}, u32[]{:S(2)}) collective-permute-start(f32[3,20,2,512]{3,2,1,0:T(2,128)S(1)} %get-tuple-element.47), channel_id=1, source_target_pairs={{0,1},{1,2},{2,3},{3,4},{4,5},{5,6},{6,7},{7,8},{8,9},{9,10},{10,1... | collective-permute-start | bytes 737288 | tf_op jit(solution)/shard_map/ppermute | solution.py:26
  (15 other events, 45.4 us)
where the time goes:
time: 656 us; the launch traced here: 648 us
  local copies, waits for them, and re-layouts  224 us (34%)
  waiting for transfers between devices  155 us (24%)
  other arithmetic  87.1 us (13%)
  matrix products  83.3 us (13%)
  starting transfers between devices  48.8 us (7%)
  blocking collectives  47.8 us (7%)
    unnamed x63, local copies, waits for them, and re-layouts  77.8 us
    all_to_all x1, blocking collectives, stokes(): spec = lax.all_to_all(spec, 'row', split_axis=2, concat_axis=4, tiled=True)  47.8 us
    all_to_all x1, waiting for transfers between devices, stokes(): spec = lax.all_to_all(spec, 'col', split_axis=3, concat_axis=4, tiled=True)  45 us
    all_to_all x1, waiting for transfers between devices, stokes(): spec = lax.all_to_all(spec, 'row', split_axis=4, concat_axis=2, tiled=True)  27.3 us
    all_to_all x1, waiting for transfers between devices, stokes(): spec = lax.all_to_all(spec, 'col', split_axis=4, concat_axis=3, tiled=True)  24.5 us
    another operation x1, local copies, waits for them, and re-layouts, stokes(): jnp.stack([jnp.einsum('cyzx,xm->cmzy', rhs, cos_x, precision=highest), -j...  19.9 us
    all_to_all x2, local copies, waits for them, and re-layouts, stokes(): spec = lax.all_to_all(spec, 'row', split_axis=2, concat_axis=4, tiled=True)  19.5 us
    all_to_all x1, waiting for transfers between devices, project(): lax.all_to_all(fixes, ('row', 'col'), split_axis=1, concat_axis=1, tiled=...  18.9 us
  transfers between devices with their start and end apart: 14, of which 12 were waited for; matrix products, arithmetic and copies ran while one was open for 14% of the time, Pallas kernels for 0%

commit v1 on v0

v1 whole, which is shorter than its diff:
```python
import functools
import math

import jax
import jax.numpy as jnp
import numpy as np
from jax import lax
from jax.experimental import pallas as pl
from jax.experimental.pallas import tpu as pltpu
from jax.sharding import PartitionSpec as P

MASS, VISC, PEN, YIELD = 0.02, 10.0, 5.0, 2.0
NPD = 72
NX, NY, NZ = 512, 128, 256
ROWS, COLS = 8, 16
CHUNKS = 4
MC = 32 // CHUNKS
F32, BF16 = jnp.float32, jnp.bfloat16
MESH = pl.DeviceIdType.MESH
HIGHEST = lax.Precision.HIGHEST
NN = (((1,), (0,)), ((), ()))
NT = (((1,), (1,)), ((), ()))

YCOMP = (3, 1, 5)
ZCOMP = (4, 5, 2)
XCOMP = (0, 3, 4)


def pieces_np(table, count):
    out = []
    rest = np.asarray(table, np.float64)
    for _ in range(count):
        piece = rest.astype(jnp.bfloat16)
        out.append(piece)
        rest = rest - piece.astype(np.float64)
    return np.stack(out)


def kron_dft(points, batch, sign):
    index = np.arange(points)
    angle = sign * 2 * np.pi * (np.outer(index, index) % points) / points
    eye = np.eye(batch)
    cos, sin = np.kron(np.cos(angle), eye), np.kron(np.sin(angle), eye)
    return np.block([[cos, sin], [-sin, cos]])


def kron_dft_z(sign):
    index = np.arange(16)
    angle = sign * 2 * np.pi * (np.outer(index, index) % 16) / 16
    eye = np.eye(8)
    cos, sin = np.kron(eye, np.cos(angle)), np.kron(eye, np.sin(angle))
    return np.block([[cos, sin], [-sin, cos]])


def mode_table():
    chunk, dest, part, inner = np.meshgrid(
        np.arange(CHUNKS), np.arange(ROWS), np.arange(2), np.arange(MC), indexing="ij"
    )
    mode = 32 * dest + MC * chunk + inner
    return mode.reshape(CHUNKS, -1), part.reshape(CHUNKS, -1)


def make_tables():
    mode, part = mode_table()
    x = np.arange(NX)
    angle = 2 * np.pi * ((mode[..., None] * x) % NX) / NX
    fwd = np.where(part[..., None] == 0, np.cos(angle), -np.sin(angle))
    weight = np.where(mode == 0, 1.0, 2.0)[..., None] / float(NX * NY * NZ)
    inv = weight * fwd
    ky_f = pieces_np(kron_dft(16, 16, -1), 2)
    ky_i = pieces_np(kron_dft(16, 16, 1), INV)
    kz_f = pieces_np(kron_dft_z(-1), 2)
    kz_i = pieces_np(kron_dft_z(1), INV)
    lane = np.arange(256)
    turn_y = 2 * np.pi * np.outer(np.arange(8), lane // 16) / NY
    turn_z = 2 * np.pi * np.outer(np.arange(16), np.arange(128) % 16) / NZ
    two_y = np.stack([np.cos(turn_y), np.sin(turn_y)]).astype(np.float32)
    two_z = np.stack([np.cos(turn_z), np.sin(turn_z)]).astype(np.float32)
    return {
        "tf": pieces_np(fwd, 2),
        "ti": pieces_np(inv, INV),
        "kyf": ky_f,
        "kyi": ky_i,
        "kzf": kz_f,
        "kzi": kz_i,
        "twy": two_y,
        "twz": two_z,
        "dz": deriv_rows(16).astype(jnp.bfloat16),
        "bz": deriv_halo().astype(jnp.bfloat16),
    }


INV = 3


def deriv_rows(lines):
    one = np.zeros((16, 16))
    for offset, coef in ((1, 8), (-1, -8), (2, -1), (-2, 1)):
        one += coef * np.eye(16, k=offset)
    return np.kron(np.eye(lines), one)


def deriv_halo():
    out = np.zeros((16, 16, 4, 16))
    for y in range(16):
        for layer, place in enumerate((-2, -1, 16, 17)):
            for z in range(16):
                out[y, z, layer, y] = {1: 8, -1: -8, 2: -1, -2: 1}.get(place - z, 0)
    return out.reshape(256, 64)


def split(value, count):
    out = []
    for step in range(count):
        piece = value.astype(BF16)
        out.append(piece)
        if step + 1 < count:
            value = value - piece.astype(F32)
    return out


def dot(a, b, dims=NN):
    return lax.dot_general(a, b, dims, preferred_element_type=F32)


def dot_exact(a, b, dims=NN):
    return lax.dot_general(a, b, dims, precision=HIGHEST, preferred_element_type=F32)


def product(a, b, dims=NN):
    count = len(a)
    total = None
    for i in range(count - 1, -1, -1):
        for j in range(count - 1 - i, -1, -1):
            term = dot(a[i], b[j], dims)
            total = term if total is None else total + term
    return total


def exact_left(a, value, count):
    total = None
    for piece in reversed(split(value, count)):
        term = dot(a, piece)
        total = term if total is None else total + term
    return total


def fft(xs, sign):
    count = len(xs)
    if count == 1:
        return xs
    even, odd = fft(xs[0::2], sign), fft(xs[1::2], sign)
    out = [None] * count
    half = count // 2
    for k in range(half):
        re, im = odd[k]
        if k == 0:
            tr, ti = re, im
        elif 4 * k == count:
            tr, ti = (-im, re) if sign > 0 else (im, -re)
        else:
            c = math.cos(2 * math.pi * k / count)
            s = sign * math.sin(2 * math.pi * k / count)
            tr, ti = re * c - im * s, re * s + im * c
        er, ei = even[k]
        out[k] = (er + tr, ei + ti)
        out[k + half] = (er - tr, ei - ti)
    return out


def along_x(field):
    axis = field.ndim - 1
    up1, up2 = pltpu.roll(field, NX - 1, axis), pltpu.roll(field, NX - 2, axis)
    lo1, lo2 = pltpu.roll(field, 1, axis), pltpu.roll(field, 2, axis)
    return (8.0 * (up1 - lo1) - (up2 - lo2)) * (1.0 / 12.0)


def centered(lo2, lo1, up1, up2):
    return (8.0 * (up1 - lo1) - (up2 - lo2)) * (1.0 / 12.0)


def kernel(
    force, mult, aux, ent, tf, ti, kyf, kyi, kzf, kzi, twy, twz, dzt, bzt,
    vext, vzh,
    yext, zf, zh, rhs, rpieces, fluid,
    x1, r1, y1, r2, z1, r3, y2, r4, ascr, bscr,
    g1, g2, g3, g4, gtile, match, geo, mgeo, hot, hott,
    halo_send, halo_recv, a_send, a_recv, g_send, g_recv,
):
    row, col = lax.axis_index("row"), lax.axis_index("col")

    def row_peer(off):
        return lax.rem(row + off, ROWS)

    def col_peer(off):
        return lax.rem(col + off, COLS)

    def remote(src, dst, send, recv, device):
        return pltpu.make_async_remote_copy(
            src_ref=src, dst_ref=dst, send_sem=send, recv_sem=recv,
            device_id=device, device_id_type=MESH,
        )

    def wait_for(ref, sem):
        pltpu.make_async_copy(ref, ref, sem).wait()

    barrier = pltpu.get_barrier_semaphore()
    for off in range(1, ROWS):
        pl.semaphore_signal(barrier, inc=1, device_id=(row_peer(off), col), device_id_type=MESH)
    for off in range(1, COLS):
        pl.semaphore_signal(barrier, inc=1, device_id=(row, col_peer(off)), device_id_type=MESH)

    def shifted(comp):
        return mult[comp] - PEN * aux[comp]

    for i, comp in enumerate(YCOMP):
        yext[i, 2:18] = shifted(comp)
    for i, comp in enumerate(ZCOMP):
        for layer, z in enumerate((0, 1, 14, 15)):
            zf[i, layer] = mult[comp, :, z, :] - PEN * aux[comp, :, z, :]
    pl.semaphore_wait(barrier, ROWS + COLS - 2)

    def halo_copies(base, ybuf, zsrc, zdst):
        up, down = (row_peer(1), col), (row_peer(ROWS - 1), col)
        right, left = (row, col_peer(1)), (row, col_peer(COLS - 1))
        sems = [(halo_send.at[base + k], halo_recv.at[base + k]) for k in range(4)]
        return [
            remote(zsrc.at[:, 2:4], zdst.at[:, 0:2], *sems[0], right),
            remote(zsrc.at[:, 0:2], zdst.at[:, 2:4], *sems[1], left),
            remote(ybuf.at[:, 16:18], ybuf.at[:, 0:2], *sems[2], up),
            remote(ybuf.at[:, 2:4], ybuf.at[:, 18:20], *sems[3], down),
        ]

    stress_halos = halo_copies(0, yext, zf, zh)
    for copy in stress_halos:
        copy.start()

    lane128 = lax.broadcasted_iota(jnp.int32, (1, 128), 1)
    entry = ent[...]
    line_of = lax.broadcasted_iota(jnp.int32, (8, 128), 0)
    gy = entry[2:3] + (row * 16).astype(F32)
    gz = entry[3:4] + (col * 16).astype(F32)
    fields = jnp.concatenate([entry[0:2], gy, gz, gy * gy, gz * gz, entry[4:6]], axis=0)
    pair = lax.broadcasted_iota(jnp.int32, (128, 128), 0)
    runs_lane = lax.broadcasted_iota(jnp.int32, (128, 128), 1)
    gather_runs = (pair // 4 == runs_lane).astype(F32)
    spread_runs = (runs_lane // 4 == pair).astype(F32)
    sums = dot_exact(fields, gather_runs)
    mean_y, mean_z = sums[2:3] * 0.25, sums[3:4] * 0.25
    inner = 4.0 * 174752.0 + 128.0 * (
        sums[4:5] - 4.0 * mean_y * mean_y + sums[5:6] - 4.0 * mean_z * mean_z
    )
    gtile[0] = jnp.concatenate(
        [sums[0:1] * 0.25, sums[1:2] * 0.25 + 63.5, mean_y, mean_z, inner, jnp.zeros((3, 128), F32)], axis=0
    )

    def gather_cols(slot, buf):
        buf[col] = gtile[slot]
        for off in range(1, COLS):
            remote(
                gtile.at[slot], buf.at[col], g_send.at[2 * slot], g_recv.at[2 * slot], (row, col_peer(off))
            ).start()

    def gather_rows(slot, buf, wide):
        wait_for(buf.at[pl.ds(0, COLS - 1)], g_recv.at[2 * slot])
        parts = []
        for q in range(4):
            total = None
            for k in range(4):
                tile = jnp.where(runs_lane[0:8] < 32, buf[4 * q + k], 0.0)
                tile = pltpu.roll(tile, 32 * k, 1) if k else tile
                total = tile if total is None else total + tile
            parts.append(total)
        wide[row] = jnp.concatenate(parts, axis=1)
        for off in range(1, ROWS):
            remote(
                wide.at[row], wide.at[row], g_send.at[2 * slot + 1], g_recv.at[2 * slot + 1], (row_peer(off), col)
            ).start()

    gather_cols(0, g1)

    for c, comp in enumerate(XCOMP):
        rhs[c] = (force[c] + along_x(shifted(comp))).reshape(256, NX)
    fluid[...] = jnp.zeros_like(fluid)
    for c, comp in enumerate(ZCOMP):
        own = shifted(comp).reshape(256, NX)
        rhs[c] += exact_left(dzt[...], own, 2) * (1.0 / 12.0)
    gather_rows(0, g1, g2)
    for copy in stress_halos:
        copy.wait_recv()
    for c in range(3):
        along_y = centered(yext[c, 0:16], yext[c, 1:17], yext[c, 3:19], yext[c, 4:20]).reshape(256, NX)
        edge = exact_left(bzt[...], zh[c].reshape(64, NX), 2) * (1.0 / 12.0)
        high, low = split(rhs[c] + along_y + edge, 2)
        rpieces[0, c] = high
        rpieces[1, c] = low

    def send_rows(stage, j, src, dst):
        dst[j, row] = src[j, row]
        for off in range(1, ROWS):
            peer = row_peer(off)
            remote(src.at[j, peer], dst.at[j, row], a_send.at[stage, j], a_recv.at[stage, j], (peer, col)).start()

    def send_cols(stage, j, src, dst):
        dst[j, col] = src[j, col]
        for off in range(1, COLS):
            peer = col_peer(off)
            remote(src.at[j, peer], dst.at[j, col], a_send.at[stage, j], a_recv.at[stage, j], (row, peer)).start()

    def await_all(stage, j, dst, count):
        wait_for(dst.at[j, pl.ds(0, count - 1)], a_recv.at[stage, j])

    def x_forward(j):
        for c in range(3):
            out = product([tf[0, j], tf[1, j]], [rpieces[0, c], rpieces[1, c]], NT)
            x1[j, :, c] = out.reshape(ROWS, 2 * MC, 256)
        send_rows(0, j, x1, r1)

    def y_forward(j):
        await_all(0, j, r1, ROWS)
        for c in range(3):
            xs = [(r1[j, s, c, 0:MC], r1[j, s, c, MC : 2 * MC]) for s in range(8)]
            for k, (re, im) in enumerate(fft(xs, -1)):
                cos, sin = twy[0, k : k + 1], twy[1, k : k + 1]
                at = k * 3 * MC + c * MC
                ascr[at : at + MC, 0:256] = re * cos + im * sin
                ascr[at : at + MC, 256:512] = im * cos - re * sin
        out = product(split(ascr[...], 2), [kyf[0], kyf[1]]).reshape(8, 3, MC, 512)
        for half in range(2):
            for part in range(2):
                at = 256 * part + 128 * half
                y1[j, pl.ds(half, 8, 2), :, part] = out[:, :, :, at : at + 128]
        send_cols(1, j, y1, r2)

    def solve(j):
        await_all(1, j, r2, COLS)
        for c in range(3):
            xs = [(r2[j, s, c, 0], r2[j, s, c, 1]) for s in range(16)]
            for k, (re, im) in enumerate(fft(xs, -1)):
                cos, sin = twz[0, k : k + 1], twz[1, k : k + 1]
                at = k * 3 * MC + c * MC
                bscr[at : at + MC, 0:128] = re * cos + im * sin
                bscr[at : at + MC, 128:256] = im * cos - re * sin
        bscr[...] = product(split(bscr[...], 2), [kzf[0], kzf[1]])
        mode = row * 32 + j * MC + lax.broadcasted_iota(jnp.int32, (MC, 128), 0)
        lanes = lax.broadcasted_iota(jnp.int32, (MC, 128), 1)
        wave_x = mode.astype(F32) * (2.0 * math.pi / NX)
        index_y = col // 2 + 8 * (8 * lax.rem(col, 2) + lanes // 16)
        wave_y = jnp.where(index_y < NY // 2, index_y, index_y - NY).astype(F32) * (2.0 * math.pi / NY)
        keep_y = (index_y != NY // 2).astype(F32)
        for k in range(16):
            index_z = k + 16 * (lanes % 16)
            wave_z = jnp.where(index_z < NZ // 2, index_z, index_z - NZ).astype(F32) * (2.0 * math.pi / NZ)
            keep = keep_y * (index_z != NZ // 2).astype(F32)
            ksq = wave_x * wave_x + wave_y * wave_y + wave_z * wave_z
            inverse = 1.0 / jnp.where(ksq > 0, ksq, 1.0)
            gain = keep / (MASS + VISC * ksq)
            for part in range(2):
                at = 3 * MC * k
                lane = slice(128 * part, 128 * part + 128)
                fx, fy, fz = (bscr[at + MC * c : at + MC * c + MC, lane] for c in range(3))
                dotk = (wave_x * fx + wave_y * fy + wave_z * fz) * inverse
                bscr[at : at + MC, lane] = (fx - wave_x * dotk) * gain
                bscr[at + MC : at + 2 * MC, lane] = (fy - wave_y * dotk) * gain
                bscr[at + 2 * MC : at + 3 * MC, lane] = (fz - wave_z * dotk) * gain
        bscr[...] = product(split(bscr[...], INV), [kzi[p] for p in range(INV)])
        for c in range(3):
            xs = []
            for k in range(16):
                cos, sin = twz[0, k : k + 1], twz[1, k : k + 1]
                at = k * 3 * MC + c * MC
                re, im = bscr[at : at + MC, 0:128], bscr[at : at + MC, 128:256]
                xs.append((re * cos - im * sin, im * cos + re * sin))
            for s, (re, im) in enumerate(fft(xs, 1)):
                z1[j, s, c, 0] = re
                z1[j, s, c, 1] = im
        send_cols(2, j, z1, r3)

    def y_inverse(j):
        await_all(2, j, r3, COLS)
        for half in range(2):
            for part in range(2):
                at = 256 * part + 128 * half
                ascr[:, at : at + 128] = r3[j, pl.ds(half, 8, 2), :, part].reshape(8 * 3 * MC, 128)
        ascr[...] = product(split(ascr[...], INV), [kyi[p] for p in range(INV)])
        for c in range(3):
            xs = []
            for k in range(8):
                cos, sin = twy[0, k : k + 1], twy[1, k : k + 1]
                at = k * 3 * MC + c * MC
                re, im = ascr[at : at + MC, 0:256], ascr[at : at + MC, 256:512]
                xs.append((re * cos - im * sin, im * cos + re * sin))
            for s, (re, im) in enumerate(fft(xs, 1)):
                y2[j, s, c, 0:MC] = re
                y2[j, s, c, MC : 2 * MC] = im
        send_rows(3, j, y2, r4)

    def x_inverse(j):
        await_all(3, j, r4, ROWS)
        for c in range(3):
            spectrum = jnp.transpose(r4[j, :, c].reshape(2 * MC * ROWS, 256))
            fluid[c] += product(split(spectrum, INV), [ti[p, j] for p in range(INV)])

    def geometry():
        wait_for(g2.at[pl.ds(0, ROWS - 1)], g_recv.at[1])
        own = dot_exact(spread_runs[0:32], fields, NT) * 0.25
        ids = own[:, 0:1]
        count = jnp.zeros((32, 1), F32)
        cx, cy, cz = count, count, count
        for r in range(ROWS):
            block = g2[r]
            same = (ids == block[0:1]).astype(F32)
            match[r] = same
            count += jnp.sum(same, axis=1, keepdims=True)
            cx += jnp.sum(same * block[1:2], axis=1, keepdims=True)
            cy += jnp.sum(same * block[2:3], axis=1, keepdims=True)
            cz += jnp.sum(same * block[3:4], axis=1, keepdims=True)
        safe = jnp.maximum(count, 1.0)
        cx, cy, cz = cx / safe, cy / safe, cz / safe
        spread = jnp.zeros((32, 1), F32)
        for r in range(ROWS):
            block = g2[r]
            dx, dy, dz = block[1:2] - cx, block[2:3] - cy, block[3:4] - cz
            inner_spread = block[4:5] + 512.0 * (dx * dx + dy * dy + dz * dz)
            spread += jnp.sum(match[r] * inner_spread, axis=1, keepdims=True)
        inertia = jnp.maximum(spread * (2.0 / 3.0), 1.0)
        place = lane128
        packed = jnp.where(place == 0, 1.0 / jnp.maximum(512.0 * count, 1.0), 0.0)
        for at, value in ((1, cx), (2, cy), (3, cz), (4, 1.0 / inertia)):
            packed = jnp.where(place == at, value, packed)
        geo[...] = packed
        mine = dot_exact((pair == runs_lane).astype(F32), fields, NT)
        centers = dot_exact(gather_runs[:, 0:32], packed)
        rel = jnp.where(place == 0, mine[:, 1:2] + 63.5 - centers[:, 1:2], 0.0)
        rel = jnp.where(place == 1, mine[:, 2:3] - centers[:, 2:3], rel)
        mgeo[...] = jnp.where(place == 2, mine[:, 3:4] - centers[:, 3:4], rel)
        rows256 = lax.broadcasted_iota(jnp.int32, (256, 128), 0).astype(F32)
        cols256 = lax.broadcasted_iota(jnp.int32, (128, 256), 1).astype(F32)
        for b in range(4):
            hot[b] = ((fields[6:7] == rows256) & (fields[7:8] == float(b))).astype(F32).astype(BF16)
            hott[b] = ((mine[:, 6:7] == cols256) & (mine[:, 7:8] == float(b))).astype(F32).astype(BF16)

    x_forward(0)
    geometry()

    @pl.loop(0, CHUNKS + 3)
    def _(t):
        pl.when(t + 1 < CHUNKS)(lambda: x_forward(t + 1))
        pl.when(t < CHUNKS)(lambda: y_forward(t))
        pl.when((t >= 1) & (t < CHUNKS + 1))(lambda: solve(t - 1))
        pl.when((t >= 2) & (t < CHUNKS + 2))(lambda: y_inverse(t - 2))
        pl.when(t >= 3)(lambda: x_inverse(t - 3))

    inside = lane128.astype(F32) - 63.5
    blocks = []
    firsts, seconds = [], []
    for c in range(3):
        block = jnp.zeros((128, 128), F32)
        for b in range(4):
            block += exact_left(hott[b], fluid[c, :, 128 * b : 128 * b + 128], 3)
        blocks.append(block)
        firsts.append(jnp.sum(block, axis=1, keepdims=True))
        seconds.append(jnp.sum(block * inside, axis=1, keepdims=True))
    rx, ry, rz = mgeo[:, 0:1], mgeo[:, 1:2], mgeo[:, 2:3]
    moments = jnp.zeros((128, 128), F32)
    for at, value in enumerate(
        (
            firsts[0],
            firsts[1],
            firsts[2],
            ry * firsts[2] - rz * firsts[1],
            rz * firsts[0] - (rx * firsts[2] + seconds[2]),
            rx * firsts[1] + seconds[1] - ry * firsts[0],
        )
    ):
        moments = jnp.where(lane128 == at, value, moments)
    gtile[1] = dot_exact(jnp.transpose(moments)[0:8], gather_runs)
    gather_cols(1, g3)
    gather_rows(1, g3, g4)
    wait_for(g4.at[pl.ds(0, ROWS - 1)], g_recv.at[3])
    totals = jnp.zeros((32, 8), F32)
    for r in range(ROWS):
        totals += dot_exact(match[r], g4[r], NT)
    packed = geo[...]
    params = jnp.zeros((32, 128), F32)
    for at in range(6):
        scale = packed[:, 0:1] if at < 3 else packed[:, 4:5]
        params = jnp.where(lane128 == at, totals[:, at : at + 1] * scale, params)
    fitted = dot_exact(gather_runs[:, 0:32], params)
    vx, vy, vz, wx, wy, wz = (fitted[:, k : k + 1] for k in range(6))
    cell_x = rx + inside
    rigid = (
        vx + wy * rz - wz * ry,
        vy + wz * cell_x - wx * rz,
        vz + wx * ry - wy * cell_x,
    )
    for c in range(3):
        fix = rigid[c] - blocks[c]
        for b in range(4):
            lanes = slice(128 * b, 128 * b + 128)
            done = fluid[c, :, lanes] + exact_left(hot[b], fix, 3)
            vext[c, 2:18, :, lanes] = done.reshape(16, 16, 128)
    for copy in stress_halos:
        copy.wait_send()
    for c in range(3):
        for layer, z in enumerate((0, 1, 14, 15)):
            zf[c, layer] = vext[c, 2:18, z, :]
    velocity_halos = halo_copies(4, vext, zf, vzh)
    for k, copy in enumerate(velocity_halos):
        copy.start()
    for copy in velocity_halos:
        copy.wait_recv()

    for copy in velocity_halos:
        copy.wait_send()
    wait_for(g1.at[pl.ds(0, COLS - 1)], g_send.at[0])
    wait_for(g2.at[pl.ds(0, ROWS - 1)], g_send.at[1])
    wait_for(g3.at[pl.ds(0, COLS - 1)], g_send.at[2])
    wait_for(g4.at[pl.ds(0, ROWS - 1)], g_send.at[3])

    @pl.loop(0, CHUNKS)
    def _(j):
        wait_for(x1.at[j, pl.ds(0, ROWS - 1)], a_send.at[0, j])
        wait_for(y1.at[j, pl.ds(0, COLS - 1)], a_send.at[1, j])
        wait_for(z1.at[j, pl.ds(0, COLS - 1)], a_send.at[2, j])
        wait_for(y2.at[j, pl.ds(0, ROWS - 1)], a_send.at[3, j])


def update(vext, vzh, mult, dzt, bzt, vel, new_aux, new_mult, *, lines):
    base = pl.program_id(0) * lines
    rows = 16 * lines
    edge = bzt[...]
    grads = []
    for c in range(3):
        field = vext[c, pl.ds(base + 2, lines)]
        vel[c] = field
        dx = along_x(field.reshape(rows, NX))
        near = [vext[c, pl.ds(base + k, lines)].reshape(rows, NX) for k in (0, 1, 3, 4)]
        dy = centered(*near)
        dz = exact_left(dzt[...], field.reshape(rows, NX), 3) + exact_left(edge, vzh[c], 3)
        grads.append((dx, dy, dz * (1.0 / 12.0)))
    strain = (
        grads[0][0],
        grads[1][1],
        grads[2][2],
        (grads[0][1] + grads[1][0]) * 0.5,
        (grads[0][2] + grads[2][0]) * 0.5,
        (grads[1][2] + grads[2][1]) * 0.5,
    )
    old = [mult[k].reshape(rows, NX) for k in range(6)]
    q = [old[k] + PEN * strain[k] for k in range(6)]
    norm = jnp.sqrt(
        q[0] * q[0] + q[1] * q[1] + q[2] * q[2] + 2.0 * (q[3] * q[3] + q[4] * q[4] + q[5] * q[5])
    )
    factor = 1.0 - YIELD / jnp.maximum(norm, YIELD)
    for k in range(6):
        aux = factor * q[k] * (1.0 / PEN)
        new_aux[k] = aux.reshape(lines, 16, NX)
        new_mult[k] = (old[k] + PEN * (strain[k] - aux)).reshape(lines, 16, NX)


def local(force, mult, aux, entry_lines, entry_owner, entry_slot):
    t = make_tables()
    particle = entry_owner[:, 0] * NPD + entry_slot
    ent = jnp.stack(
        [
            particle,
            (entry_lines % 4) * 128,
            entry_lines // 64,
            entry_lines // 4 % 16,
            entry_lines // 4,
            entry_lines % 4,
            jnp.zeros_like(entry_lines),
            jnp.zeros_like(entry_lines),
        ]
    ).astype(F32)
    vm = pl.BlockSpec(memory_space=pltpu.VMEM)
    sems = pltpu.SemaphoreType.DMA
    names = ("tf", "ti", "kyf", "kyi", "kzf", "kzi", "twy", "twz", "dz", "bz")
    scratch = [
        pltpu.VMEM((3, 20, 16, NX), F32),
        pltpu.VMEM((3, 4, 16, NX), F32),
        pltpu.VMEM((3, 4, 16, NX), F32),
        pltpu.VMEM((3, 256, NX), F32),
        pltpu.VMEM((2, 3, 256, NX), BF16),
        pltpu.VMEM((3, 256, NX), F32),
        pltpu.VMEM((CHUNKS, ROWS, 3, 2 * MC, 256), F32),
        pltpu.VMEM((CHUNKS, ROWS, 3, 2 * MC, 256), F32),
        pltpu.VMEM((CHUNKS, COLS, 3, 2, MC, 128), F32),
        pltpu.VMEM((CHUNKS, COLS, 3, 2, MC, 128), F32),
        pltpu.VMEM((CHUNKS, COLS, 3, 2, MC, 128), F32),
        pltpu.VMEM((CHUNKS, COLS, 3, 2, MC, 128), F32),
        pltpu.VMEM((CHUNKS, ROWS, 3, 2 * MC, 256), F32),
        pltpu.VMEM((CHUNKS, ROWS, 3, 2 * MC, 256), F32),
        pltpu.VMEM((24 * MC, 512), F32),
        pltpu.VMEM((48 * MC, 256), F32),
        pltpu.VMEM((COLS, 8, 128), F32),
        pltpu.VMEM((ROWS, 8, 512), F32),
        pltpu.VMEM((COLS, 8, 128), F32),
        pltpu.VMEM((ROWS, 8, 512), F32),
        pltpu.VMEM((2, 8, 128), F32),
        pltpu.VMEM((ROWS, 32, 512), F32),
        pltpu.VMEM((32, 128), F32),
        pltpu.VMEM((128, 128), F32),
        pltpu.VMEM((4, 256, 128), BF16),
        pltpu.VMEM((4, 128, 256), BF16),
        sems((8,)),
        sems((8,)),
        sems((4, CHUNKS)),
        sems((4, CHUNKS)),
        sems((4,)),
        sems((4,)),
    ]
    vext, vzh = pl.pallas_call(
        kernel,
        out_shape=(
            jax.ShapeDtypeStruct((3, 20, 16, NX), F32),
            jax.ShapeDtypeStruct((3, 4, 16, NX), F32),
        ),
        in_specs=[vm] * (4 + len(names)),
        out_specs=(vm, vm),
        scratch_shapes=scratch,
        compiler_params=pltpu.CompilerParams(
            collective_id=0, has_side_effects=True, vmem_limit_bytes=60 * 2**20
        ),
    )(force, mult, aux, ent, *(jnp.asarray(t[k]) for k in names))

    lines = 4
    whole = lambda *shape: pl.BlockSpec(shape, lambda i: (0,) * len(shape))
    part = lambda n: pl.BlockSpec((n, lines, 16, NX), lambda i: (0, i, 0, 0))
    return tuple(
        pl.pallas_call(
            functools.partial(update, lines=lines),
            grid=(16 // lines,),
            out_shape=tuple(jax.ShapeDtypeStruct((n, 16, 16, NX), F32) for n in (3, 6, 6)),
            in_specs=[
                whole(3, 20, 16, NX),
                whole(3, 64, NX),
                part(6),
                whole(16 * lines, 16 * lines),
                pl.BlockSpec((16 * lines, 64), lambda i: (i, 0)),
            ],
            out_specs=tuple(part(n) for n in (3, 6, 6)),
            compiler_params=pltpu.CompilerParams(vmem_limit_bytes=48 * 2**20),
        )(
            vext,
            vzh.reshape(3, 64, NX),
            mult,
            jnp.asarray(deriv_rows(lines).astype(jnp.bfloat16)),
            jnp.asarray(t["bz"]),
        )
    )


def solution(mesh):
    field = P(None, "row", "col", None)
    return jax.shard_map(
        local,
        mesh=mesh,
        in_specs=(field, field, field, P(("row", "col")), P(("row", "col"), None), P(("row", "col"))),
        out_specs=(field, field, field),
        check_vma=False,
    )
```

time: 656 us -> 110 us (0.17); the launches traced: 648 us -> 110 us
  local copies, waits for them, and re-layouts: 224 us -> 2.57 us
  waiting for transfers between devices: 155 us -> 0 us
  Pallas kernels: 0 us -> 104 us
  other arithmetic: 87.1 us -> 2.61 us
  matrix products: 83.3 us -> 0 us
  starting transfers between devices: 48.8 us -> 0 us
  blocking collectives: 47.8 us -> 0 us
    all_to_all x6 -> x0, waiting for transfers between devices: 134 us -> none  [the longest x1 45 us: stokes(): spec = lax.all_to_all(spec, 'col', split_axis=3, concat_axis=4, tiled=True)]
    pallas_call x0 -> x2, Pallas kernels: none -> 104 us  [the longest x1 98.7 us: local(): pl.pallas_call(kernel, out_shape=(jax.ShapeDtypeStruct((3, 20, 16, NX), F...]
    unnamed x63 -> x10, local copies, waits for them, and re-layouts: 77.8 us -> 2.54 us
    dot_general x22 -> x0, matrix products: 65.3 us -> none  [the longest x2 8.72 us: forward_pair(): jnp.einsum(form, real_part, cosines, precision=highest)]
    all_to_all x1 -> x0, blocking collectives: 47.8 us -> none  [stokes(): spec = lax.all_to_all(spec, 'row', split_axis=2, concat_axis=4, tiled=True)]
    all_to_all x4 -> x0, other arithmetic: 43.5 us -> none  [the longest x1 11.3 us: stokes(): spec = lax.all_to_all(spec, 'row', split_axis=4, concat_axis=2, tiled=True)]
    another operation x10 -> x2, local copies, waits for them, and re-layouts: 38.8 us -> 0.03 us  [local(): jnp.stack([particle, entry_lines % 4 * 128, entry_lines // 64, entry_line...]
    all_to_all x6 -> x0, starting transfers between devices: 36.6 us -> none  [the longest x1 9.58 us: project(): lax.all_to_all(meta, ('row', 'col'), split_axis=1, concat_axis=1, tiled=T...]
  transfers between devices with their start and end apart: 14 -> 0, of which waited for: 12 -> 0; matrix products, arithmetic and copies ran while one was open for 14% -> 0% of each run, Pallas kernels for 0% -> 0%
where the time goes in v1:
time: 110 us
  Pallas kernels  104 us (95%)
  other arithmetic  2.61 us (2%)
  local copies, waits for them, and re-layouts  2.57 us (2%)
    pallas_call x1, Pallas kernels, local(): pl.pallas_call(kernel, out_shape=(jax.ShapeDtypeStruct((3, 20, 16, NX), F...  98.7 us
    pallas_call x1, Pallas kernels, local(): pl.pallas_call(functools.partial(update, lines=lines), grid=(16 // lines,...  5.59 us
    unnamed x10, local copies, waits for them, and re-layouts  2.54 us

profile of v1, /device:TPU:1, one launch (start us, length us, event | category | flops | bytes accessed | tf_op | source)
XLA Modules:
  0.0 110.2 jit_solution(5899933393289072591)
XLA Ops:
  0.6 0.7 fusion.2
  1.3 0.7 fusion.4
  2.0 0.7 fusion
  2.7 0.6 convert_element_type.3.ent
  3.3 0.0 copy-start
  3.3 0.0 copy-start.3
  3.3 0.0 copy-start.4
  3.3 98.7 %shard_map.184 = (f32[3,20,16,512]{3,2,1,0:T(8,128)}, f32[3,4,16,512]{3,2,1,0:T(8,128)}) custom-call(f32[3,16,16,512]{3,2,1,0:T(8,128)} %force.1, f32[6,16,16,512]{3,2,1,0:T(8,128)} %mult.3, f32[6,16,16,512]{3,2,1,0:T(8,128)} %aux.1, f32[8,128]{1,0:T(8,128)} %convert_element_type.3.ent, bf16[2,4,128,512]{3,2,1,0:T(8,128)(2,1)} %constant.82.clone.tf, ...), custom_call_target="tpu_custom_call" | custom-call | tf_op jit(solution)/shard_map/pallas_call | solution.py:614
  102.0 0.0 copy-done
  102.0 0.0 copy-done.3
  102.0 0.0 copy-done.4
  102.1 0.0 copy-start.1
  102.1 1.5 %copy-done.1 = f32[3,20,16,512]{3,2,1,0:T(8,128)S(1)} copy-done((f32[3,20,16,512]{3,2,1,0:T(8,128)S(1)}, f32[3,20,16,512]{3,2,1,0:T(8,128)}, u32[]{:S(2)}) %copy-start.1) | copy-done | bytes 1966104
  103.6 0.0 copy-start.2
  103.6 1.0 copy-done.2
  104.6 5.6 %shard_map.185 = (f32[3,16,16,512]{3,2,1,0:T(8,128)}, f32[6,16,16,512]{3,2,1,0:T(8,128)}, f32[6,16,16,512]{3,2,1,0:T(8,128)}) custom-call(f32[3,20,16,512]{3,2,1,0:T(8,128)S(1)} %copy-done.1, f32[3,64,512]{2,1,0:T(8,128)S(1)} %bitcast.16, f32[6,16,16,512]{3,2,1,0:T(8,128)S(1)} %copy-done, bf16[64,64]{1,0:T(8,128)(2,1)S(1)} %copy-done.4, ...), custom_call_target="tpu_custom_call" | custom-call | tf_op jit(solution)/shard_map/pallas_call | solution.py:632
  (2 shorter events, 0.0 us)
Async XLA Ops:
  3.3 98.7 %copy-start = (f32[6,16,16,512]{3,2,1,0:T(8,128)S(1)}, f32[6,16,16,512]{3,2,1,0:T(8,128)}, u32[]{:S(2)}) copy-start(f32[6,16,16,512]{3,2,1,0:T(8,128)} %mult.3) | copy-start | bytes 9437188
  3.3 98.8 %copy-start.3 = (bf16[256,64]{1,0:T(8,128)(2,1)S(1)}, bf16[256,64]{1,0:T(8,128)(2,1)}, u32[]{:S(2)}) copy-start(bf16[256,64]{1,0:T(8,128)(2,1)} %constant.91.clone.bzt) | copy-start | bytes 98308
  3.3 98.8 %copy-start.4 = (bf16[64,64]{1,0:T(8,128)(2,1)S(1)}, bf16[64,64]{1,0:T(8,128)(2,1)}, u32[]{:S(2)}) copy-start(bf16[64,64]{1,0:T(8,128)(2,1)} %constant.92.clone.dzt) | copy-start | bytes 24580
  102.1 1.5 %copy-start.1 = (f32[3,20,16,512]{3,2,1,0:T(8,128)S(1)}, f32[3,20,16,512]{3,2,1,0:T(8,128)}, u32[]{:S(2)}) copy-start(f32[3,20,16,512]{3,2,1,0:T(8,128)} %get-tuple-element.5.vext) | copy-start | bytes 5898244
  103.6 1.0 copy-start.2

commit v2 on v1

--- a/solution.py
+++ b/solution.py
@@ -20,6 +20,11 @@
 HIGHEST = lax.Precision.HIGHEST
 NN = (((1,), (0,)), ((), ()))
 NT = (((1,), (1,)), ((), ()))
+
+FAR = (
+    (2, 2), (2, 1), (1, 2), (2, 3), (3, 2), (1, 1), (3, 3), (1, 3), (3, 1),
+    (2, 0), (0, 2), (1, 0), (0, 1), (3, 0), (0, 3),
+)
 
 YCOMP = (3, 1, 5)
 ZCOMP = (4, 5, 2)
@@ -180,12 +185,14 @@
 
 
 def kernel(
-    force, mult, aux, ent, tf, ti, kyf, kyi, kzf, kzi, twy, twz, dzt, bzt,
+    force_in, mult_in, aux_in, lines_in, owner_in, slot_in,
+    tf_in, ti_in, kyf_in, kyi_in, kzf_in, kzi_in, twy_in, twz_in, dzt_in, bzt_in,
     vext, vzh,
+    force, mult, aux, tf, ti, kyf, kyi, kzf, kzi, twy, twz, dzt, bzt,
     yext, zf, zh, rhs, rpieces, fluid,
     x1, r1, y1, r2, z1, r3, y2, r4, ascr, bscr,
     g1, g2, g3, g4, gtile, match, geo, mgeo, hot, hott,
-    halo_send, halo_recv, a_send, a_recv, g_send, g_recv,
+    halo_send, halo_recv, a_send, a_recv, g_send, g_recv, load_sem,
 ):
     row, col = lax.axis_index("row"), lax.axis_index("col")
 
@@ -204,6 +211,30 @@
     def wait_for(ref, sem):
         pltpu.make_async_copy(ref, ref, sem).wait()
 
+    loads = {}
+
+    def load(name, src, dst):
+        loads[name] = pltpu.make_async_copy(src, dst, load_sem.at[len(loads)])
+        loads[name].start()
+
+    for comp in (3, 1, 5, 4, 2):
+        load(("mult", comp), mult_in.at[comp], mult.at[comp])
+        load(("aux", comp), aux_in.at[comp], aux.at[comp])
+    load("dzt", dzt_in, dzt)
+    load("bzt", bzt_in, bzt)
+    load(("mult", 0), mult_in.at[0], mult.at[0])
+    load(("aux", 0), aux_in.at[0], aux.at[0])
+    load("force", force_in, force)
+    for name, src, dst in (
+        ("tf", tf_in, tf), ("twy", twy_in, twy), ("kyf", kyf_in, kyf), ("twz", twz_in, twz),
+        ("kzf", kzf_in, kzf), ("kzi", kzi_in, kzi), ("kyi", kyi_in, kyi), ("ti", ti_in, ti),
+    ):
+        load(name, src, dst)
+
+    def loaded(*names):
+        for name in names:
+            loads.pop(name).wait()
+
     barrier = pltpu.get_barrier_semaphore()
     for off in range(1, ROWS):
         pl.semaphore_signal(barrier, inc=1, device_id=(row_peer(off), col), device_id_type=MESH)
@@ -214,7 +245,9 @@
         return mult[comp] - PEN * aux[comp]
 
     for i, comp in enumerate(YCOMP):
+        loaded(("mult", comp), ("aux", comp))
         yext[i, 2:18] = shifted(comp)
+    loaded(("mult", 4), ("aux", 4), ("mult", 2), ("aux", 2))
     for i, comp in enumerate(ZCOMP):
         for layer, z in enumerate((0, 1, 14, 15)):
             zf[i, layer] = mult[comp, :, z, :] - PEN * aux[comp, :, z, :]
@@ -236,11 +269,23 @@
         copy.start()
 
     lane128 = lax.broadcasted_iota(jnp.int32, (1, 128), 1)
-    entry = ent[...]
-    line_of = lax.broadcasted_iota(jnp.int32, (8, 128), 0)
-    gy = entry[2:3] + (row * 16).astype(F32)
-    gz = entry[3:4] + (col * 16).astype(F32)
-    fields = jnp.concatenate([entry[0:2], gy, gz, gy * gy, gz * gz, entry[4:6]], axis=0)
+    lines, block_x = lines_in[...], lines_in[...] & 3
+    particle = owner_in[...] * NPD + slot_in[...]
+    gy = ((lines >> 6) + row * 16).astype(F32)
+    gz = (((lines >> 2) & 15) + col * 16).astype(F32)
+    fields = jnp.concatenate(
+        [
+            particle.astype(F32),
+            (block_x * 128).astype(F32),
+            gy,
+            gz,
+            gy * gy,
+            gz * gz,
+            (lines >> 2).astype(F32),
+            block_x.astype(F32),
+        ],
+        axis=0,
+    )
     pair = lax.broadcasted_iota(jnp.int32, (128, 128), 0)
     runs_lane = lax.broadcasted_iota(jnp.int32, (128, 128), 1)
     gather_runs = (pair // 4 == runs_lane).astype(F32)
@@ -279,6 +324,7 @@
 
     gather_cols(0, g1)
 
+    loaded("dzt", "bzt", ("mult", 0), ("aux", 0), "force")
     for c, comp in enumerate(XCOMP):
         rhs[c] = (force[c] + along_x(shifted(comp))).reshape(256, NX)
     fluid[...] = jnp.zeros_like(fluid)
@@ -303,8 +349,8 @@
 
     def send_cols(stage, j, src, dst):
         dst[j, col] = src[j, col]
-        for off in range(1, COLS):
-            peer = col_peer(off)
+        for dy, dz in FAR:
+            peer = 4 * lax.rem(col // 4 + dz, 4) + lax.rem(col % 4 + dy, 4)
             remote(src.at[j, peer], dst.at[j, col], a_send.at[stage, j], a_recv.at[stage, j], (row, peer)).start()
 
     def await_all(stage, j, dst, count):
@@ -440,16 +486,19 @@
             hot[b] = ((fields[6:7] == rows256) & (fields[7:8] == float(b))).astype(F32).astype(BF16)
             hott[b] = ((mine[:, 6:7] == cols256) & (mine[:, 7:8] == float(b))).astype(F32).astype(BF16)
 
+    loaded("tf")
     x_forward(0)
+    x_forward(1)
     geometry()
-
-    @pl.loop(0, CHUNKS + 3)
+    loaded("twy", "kyf", "twz", "kzf", "kzi", "kyi", "ti")
+
+    @pl.loop(0, CHUNKS + 5)
     def _(t):
-        pl.when(t + 1 < CHUNKS)(lambda: x_forward(t + 1))
         pl.when(t < CHUNKS)(lambda: y_forward(t))
-        pl.when((t >= 1) & (t < CHUNKS + 1))(lambda: solve(t - 1))
-        pl.when((t >= 2) & (t < CHUNKS + 2))(lambda: y_inverse(t - 2))
-        pl.when(t >= 3)(lambda: x_inverse(t - 3))
+        pl.when(t + 2 < CHUNKS)(lambda: x_forward(t + 2))
+        pl.when((t >= 2) & (t < CHUNKS + 2))(lambda: solve(t - 2))
+        pl.when((t >= 4) & (t < CHUNKS + 4))(lambda: y_inverse(t - 4))
+        pl.when(t >= 5)(lambda: x_inverse(t - 5))
 
     inside = lane128.astype(F32) - 63.5
     blocks = []
@@ -561,23 +610,12 @@
 
 def local(force, mult, aux, entry_lines, entry_owner, entry_slot):
     t = make_tables()
-    particle = entry_owner[:, 0] * NPD + entry_slot
-    ent = jnp.stack(
-        [
-            particle,
-            (entry_lines % 4) * 128,
-            entry_lines // 64,
-            entry_lines // 4 % 16,
-            entry_lines // 4,
-            entry_lines % 4,
-            jnp.zeros_like(entry_lines),
-            jnp.zeros_like(entry_lines),
-        ]
-    ).astype(F32)
     vm = pl.BlockSpec(memory_space=pltpu.VMEM)
+    hbm = pl.BlockSpec(memory_space=pltpu.HBM)
     sems = pltpu.SemaphoreType.DMA
     names = ("tf", "ti", "kyf", "kyi", "kzf", "kzi", "twy", "twz", "dz", "bz")
-    scratch = [
+    loads = [force, mult, aux] + [jnp.asarray(t[k]) for k in names]
+    scratch = [pltpu.VMEM(a.shape, a.dtype) for a in loads] + [
         pltpu.VMEM((3, 20, 16, NX), F32),
         pltpu.VMEM((3, 4, 16, NX), F32),
         pltpu.VMEM((3, 4, 16, NX), F32),
@@ -610,6 +648,7 @@
         sems((4, CHUNKS)),
         sems((4,)),
         sems((4,)),
+        sems((len(names) + 13,)),
     ]
     vext, vzh = pl.pallas_call(
         kernel,
@@ -617,13 +656,21 @@
             jax.ShapeDtypeStruct((3, 20, 16, NX), F32),
             jax.ShapeDtypeStruct((3, 4, 16, NX), F32),
         ),
-        in_specs=[vm] * (4 + len(names)),
+        in_specs=[hbm] * 3 + [vm] * 3 + [hbm] * len(names),
         out_specs=(vm, vm),
         scratch_shapes=scratch,
         compiler_params=pltpu.CompilerParams(
-            collective_id=0, has_side_effects=True, vmem_limit_bytes=60 * 2**20
+            collective_id=0, has_side_effects=True, vmem_limit_bytes=58 * 2**20
         ),
-    )(force, mult, aux, ent, *(jnp.asarray(t[k]) for k in names))
+    )(
+        force,
+        mult,
+        aux,
+        entry_lines.reshape(1, 128),
+        entry_owner.reshape(1, 128),
+        entry_slot.reshape(1, 128),
+        *loads[3:],
+    )
 
     lines = 4
     whole = lambda *shape: pl.BlockSpec(shape, lambda i: (0,) * len(shape))
@@ -641,7 +688,7 @@
                 pl.BlockSpec((16 * lines, 64), lambda i: (i, 0)),
             ],
             out_specs=tuple(part(n) for n in (3, 6, 6)),
-            compiler_params=pltpu.CompilerParams(vmem_limit_bytes=48 * 2**20),
+            compiler_params=pltpu.CompilerParams(vmem_limit_bytes=58 * 2**20),
         )(
             vext,
             vzh.reshape(3, 64, NX),

time: 110 us -> 105 us (0.955)
  other arithmetic: 2.61 us -> 0 us
  local copies, waits for them, and re-layouts: 2.57 us -> 0 us
    unnamed x10 -> x0, local copies, waits for them, and re-layouts: 2.54 us -> none
    pallas_call x1, Pallas kernels: 98.7 us -> 96.2 us  [local(): pl.pallas_call(kernel, out_shape=(jax.ShapeDtypeStruct((3, 20, 16, NX), F...]
    pallas_call x1, Pallas kernels: 5.59 us -> 8.08 us  [local(): pl.pallas_call(functools.partial(update, lines=lines), grid=(16 // lines,...]
    another operation x3 -> x0, other arithmetic: 2.01 us -> none  [local(): jnp.stack([particle, entry_lines % 4 * 128, entry_lines // 64, entry_line...]
where the time goes in v2:
time: 105 us
  Pallas kernels  104 us (99%)
    pallas_call x1, Pallas kernels, local(): pl.pallas_call(kernel, out_shape=(jax.ShapeDtypeStruct((3, 20, 16, NX), F...  96.2 us
    pallas_call x1, Pallas kernels, local(): pl.pallas_call(functools.partial(update, lines=lines), grid=(16 // lines,...  8.08 us

profile of v2, /device:TPU:1, one launch (start us, length us, event | category | flops | bytes accessed | tf_op | source)
XLA Modules:
  0.0 104.9 jit_solution(4534483035179736739)
XLA Ops:
  0.6 96.2 %shard_map.184 = (f32[3,20,16,512]{3,2,1,0:T(8,128)}, f32[3,4,16,512]{3,2,1,0:T(8,128)}) custom-call(f32[3,16,16,512]{3,2,1,0:T(8,128)} %force_in.1, f32[6,16,16,512]{3,2,1,0:T(8,128)} %mult.1, f32[6,16,16,512]{3,2,1,0:T(8,128)} %aux_in.1, s32[1,128]{1,0:T(1,128)} %bitcast.5, s32[1,128]{1,0:T(1,128)} %bitcast.6, s32[1,128]{1,0:T(1,128)} %bitcast.7, ...), custom_call_target="tpu_custom_call" | custom-call | tf_op jit(solution)/shard_map/pallas_call | solution.py:653
  96.9 8.1 %shard_map.185 = (f32[3,16,16,512]{3,2,1,0:T(8,128)}, f32[6,16,16,512]{3,2,1,0:T(8,128)}, f32[6,16,16,512]{3,2,1,0:T(8,128)}) custom-call(f32[3,20,16,512]{3,2,1,0:T(8,128)} %get-tuple-element.5.vext, f32[3,64,512]{2,1,0:T(8,128)} %bitcast.4, f32[6,16,16,512]{3,2,1,0:T(8,128)} %mult.1, bf16[64,64]{1,0:T(8,128)(2,1)} %constant.32.clone.dzt, ...), custom_call_target="tpu_custom_call" | custom-call | tf_op jit(solution)/shard_map/pallas_call | solution.py:679

commit v3 on v2

--- a/solution.py
+++ b/solution.py
@@ -187,12 +187,12 @@
 def kernel(
     force_in, mult_in, aux_in, lines_in, owner_in, slot_in,
     tf_in, ti_in, kyf_in, kyi_in, kzf_in, kzi_in, twy_in, twz_in, dzt_in, bzt_in,
-    vext, vzh,
+    vext_out, vzh_out,
     force, mult, aux, tf, ti, kyf, kyi, kzf, kzi, twy, twz, dzt, bzt,
-    yext, zf, zh, rhs, rpieces, fluid,
+    yext, zf, zh, vext, vzh, rhs, rpieces, fluid,
     x1, r1, y1, r2, z1, r3, y2, r4, ascr, bscr,
     g1, g2, g3, g4, gtile, match, geo, mgeo, hot, hott,
-    halo_send, halo_recv, a_send, a_recv, g_send, g_recv, load_sem,
+    halo_send, halo_recv, a_send, a_recv, g_send, g_recv, load_sem, store_sem,
 ):
     row, col = lax.axis_index("row"), lax.axis_index("col")
 
@@ -217,7 +217,7 @@
         loads[name] = pltpu.make_async_copy(src, dst, load_sem.at[len(loads)])
         loads[name].start()
 
-    for comp in (3, 1, 5, 4, 2):
+    for comp in (4, 5, 2, 3, 1):
         load(("mult", comp), mult_in.at[comp], mult.at[comp])
         load(("aux", comp), aux_in.at[comp], aux.at[comp])
     load("dzt", dzt_in, dzt)
@@ -244,11 +244,8 @@
     def shifted(comp):
         return mult[comp] - PEN * aux[comp]
 
-    for i, comp in enumerate(YCOMP):
+    for i, comp in enumerate(ZCOMP):
         loaded(("mult", comp), ("aux", comp))
-        yext[i, 2:18] = shifted(comp)
-    loaded(("mult", 4), ("aux", 4), ("mult", 2), ("aux", 2))
-    for i, comp in enumerate(ZCOMP):
         for layer, z in enumerate((0, 1, 14, 15)):
             zf[i, layer] = mult[comp, :, z, :] - PEN * aux[comp, :, z, :]
     pl.semaphore_wait(barrier, ROWS + COLS - 2)
@@ -265,7 +262,13 @@
         ]
 
     stress_halos = halo_copies(0, yext, zf, zh)
-    for copy in stress_halos:
+    for copy in stress_halos[0:2]:
+        copy.start()
+    for i, comp in enumerate(YCOMP):
+        if comp != 5:
+            loaded(("mult", comp), ("aux", comp))
+        yext[i, 2:18] = shifted(comp)
+    for copy in stress_halos[2:4]:
         copy.start()
 
     lane128 = lax.broadcasted_iota(jnp.int32, (1, 128), 1)
@@ -555,10 +558,21 @@
         for layer, z in enumerate((0, 1, 14, 15)):
             zf[c, layer] = vext[c, 2:18, z, :]
     velocity_halos = halo_copies(4, vext, zf, vzh)
-    for k, copy in enumerate(velocity_halos):
+    for copy in velocity_halos:
         copy.start()
+    stores = [pltpu.make_async_copy(vext.at[c, 2:18], vext_out.at[c, 2:18], store_sem.at[c]) for c in range(3)]
+    for store in stores:
+        store.start()
     for copy in velocity_halos:
         copy.wait_recv()
+    late = [
+        pltpu.make_async_copy(vext.at[:, 0:2], vext_out.at[:, 0:2], store_sem.at[3]),
+        pltpu.make_async_copy(vext.at[:, 18:20], vext_out.at[:, 18:20], store_sem.at[4]),
+        pltpu.make_async_copy(vzh, vzh_out, store_sem.at[5]),
+    ]
+    for store in late:
+        store.start()
+    stores += late
 
     for copy in velocity_halos:
         copy.wait_send()
@@ -574,17 +588,20 @@
         wait_for(z1.at[j, pl.ds(0, COLS - 1)], a_send.at[2, j])
         wait_for(y2.at[j, pl.ds(0, ROWS - 1)], a_send.at[3, j])
 
-
-def update(vext, vzh, mult, dzt, bzt, vel, new_aux, new_mult, *, lines):
-    base = pl.program_id(0) * lines
+    for store in stores:
+        store.wait()
+
+
+def update(vlow, vhigh, vzh, mult, dzt, bzt, vel, new_aux, new_mult, *, lines):
     rows = 16 * lines
     edge = bzt[...]
     grads = []
     for c in range(3):
-        field = vext[c, pl.ds(base + 2, lines)]
+        both = jnp.concatenate([vlow[c], vhigh[c]], axis=0)
+        field = both[2 : lines + 2]
         vel[c] = field
         dx = along_x(field.reshape(rows, NX))
-        near = [vext[c, pl.ds(base + k, lines)].reshape(rows, NX) for k in (0, 1, 3, 4)]
+        near = [both[k : lines + k].reshape(rows, NX) for k in (0, 1, 3, 4)]
         dy = centered(*near)
         dz = exact_left(dzt[...], field.reshape(rows, NX), 3) + exact_left(edge, vzh[c], 3)
         grads.append((dx, dy, dz * (1.0 / 12.0)))
@@ -618,6 +635,8 @@
     scratch = [pltpu.VMEM(a.shape, a.dtype) for a in loads] + [
         pltpu.VMEM((3, 20, 16, NX), F32),
         pltpu.VMEM((3, 4, 16, NX), F32),
+        pltpu.VMEM((3, 4, 16, NX), F32),
+        pltpu.VMEM((3, 20, 16, NX), F32),
         pltpu.VMEM((3, 4, 16, NX), F32),
         pltpu.VMEM((3, 256, NX), F32),
         pltpu.VMEM((2, 3, 256, NX), BF16),
@@ -649,6 +668,7 @@
         sems((4,)),
         sems((4,)),
         sems((len(names) + 13,)),
+        sems((6,)),
     ]
     vext, vzh = pl.pallas_call(
         kernel,
@@ -657,7 +677,7 @@
             jax.ShapeDtypeStruct((3, 4, 16, NX), F32),
         ),
         in_specs=[hbm] * 3 + [vm] * 3 + [hbm] * len(names),
-        out_specs=(vm, vm),
+        out_specs=(hbm, hbm),
         scratch_shapes=scratch,
         compiler_params=pltpu.CompilerParams(
             collective_id=0, has_side_effects=True, vmem_limit_bytes=58 * 2**20
@@ -681,7 +701,8 @@
             grid=(16 // lines,),
             out_shape=tuple(jax.ShapeDtypeStruct((n, 16, 16, NX), F32) for n in (3, 6, 6)),
             in_specs=[
-                whole(3, 20, 16, NX),
+                part(3),
+                pl.BlockSpec((3, lines, 16, NX), lambda i: (0, i + 1, 0, 0)),
                 whole(3, 64, NX),
                 part(6),
                 whole(16 * lines, 16 * lines),
@@ -691,6 +712,7 @@
             compiler_params=pltpu.CompilerParams(vmem_limit_bytes=58 * 2**20),
         )(
             vext,
+            vext,
             vzh.reshape(3, 64, NX),
             mult,
             jnp.asarray(deriv_rows(lines).astype(jnp.bfloat16)),

time: 105 us -> 105 us (level)
  no operation moved by 1% of the time
where the time goes in v3:
time: 105 us
  Pallas kernels  104 us (99%)
    pallas_call x1, Pallas kernels, local(): pl.pallas_call(kernel, out_shape=(jax.ShapeDtypeStruct((3, 20, 16, NX), F...  96.2 us
    pallas_call x1, Pallas kernels, local(): pl.pallas_call(functools.partial(update, lines=lines), grid=(16 // lines,...  8.19 us

profile of v3, /device:TPU:1, one launch (start us, length us, event | category | flops | bytes accessed | tf_op | source)
XLA Modules:
  0.0 105.0 jit_solution(12738581243782868745)
XLA Ops:
  0.6 96.2 %shard_map.184 = (f32[3,20,16,512]{3,2,1,0:T(8,128)}, f32[3,4,16,512]{3,2,1,0:T(8,128)}) custom-call(f32[3,16,16,512]{3,2,1,0:T(8,128)} %force_in.1, f32[6,16,16,512]{3,2,1,0:T(8,128)} %mult.1, f32[6,16,16,512]{3,2,1,0:T(8,128)} %aux_in.1, s32[1,128]{1,0:T(1,128)} %bitcast.5, s32[1,128]{1,0:T(1,128)} %bitcast.6, s32[1,128]{1,0:T(1,128)} %bitcast.7, ...), custom_call_target="tpu_custom_call" | custom-call | tf_op jit(solution)/shard_map/pallas_call | solution.py:673
  96.8 8.2 %shard_map.185 = (f32[3,16,16,512]{3,2,1,0:T(8,128)}, f32[6,16,16,512]{3,2,1,0:T(8,128)}, f32[6,16,16,512]{3,2,1,0:T(8,128)}) custom-call(f32[3,20,16,512]{3,2,1,0:T(8,128)} %get-tuple-element.5.vlow.vhigh, f32[3,20,16,512]{3,2,1,0:T(8,128)} %get-tuple-element.5.vlow.vhigh, f32[3,64,512]{2,1,0:T(8,128)} %bitcast.4, f32[6,16,16,512]{3,2,1,0:T(8,128)} %mult.1, ...), custom_call_target="tpu_custom_call" | custom-call | tf_op jit(solution)/shard_map/pallas_call | solution.py:699

commit v4 on v3

--- a/solution.py
+++ b/solution.py
@@ -191,7 +191,7 @@
     force, mult, aux, tf, ti, kyf, kyi, kzf, kzi, twy, twz, dzt, bzt,
     yext, zf, zh, vext, vzh, rhs, rpieces, fluid,
     x1, r1, y1, r2, z1, r3, y2, r4, ascr, bscr,
-    g1, g2, g3, g4, gtile, match, geo, mgeo, hot, hott,
+    g1, g2, g3, g4, gtile, match, mgeo, hot, hott, nbtile, nbcol, nbhot, nbkeep,
     halo_send, halo_recv, a_send, a_recv, g_send, g_recv, load_sem, store_sem,
 ):
     row, col = lax.axis_index("row"), lax.axis_index("col")
@@ -250,18 +250,18 @@
             zf[i, layer] = mult[comp, :, z, :] - PEN * aux[comp, :, z, :]
     pl.semaphore_wait(barrier, ROWS + COLS - 2)
 
-    def halo_copies(base, ybuf, zsrc, zdst):
+    def halo_copies(base, ysrc, high, low, ydst, zsrc, zdst):
         up, down = (row_peer(1), col), (row_peer(ROWS - 1), col)
         right, left = (row, col_peer(1)), (row, col_peer(COLS - 1))
         sems = [(halo_send.at[base + k], halo_recv.at[base + k]) for k in range(4)]
         return [
             remote(zsrc.at[:, 2:4], zdst.at[:, 0:2], *sems[0], right),
             remote(zsrc.at[:, 0:2], zdst.at[:, 2:4], *sems[1], left),
-            remote(ybuf.at[:, 16:18], ybuf.at[:, 0:2], *sems[2], up),
-            remote(ybuf.at[:, 2:4], ybuf.at[:, 18:20], *sems[3], down),
+            remote(ysrc.at[:, high : high + 2], ydst.at[:, 0:2], *sems[2], up),
+            remote(ysrc.at[:, low : low + 2], ydst.at[:, 18:20], *sems[3], down),
         ]
 
-    stress_halos = halo_copies(0, yext, zf, zh)
+    stress_halos = halo_copies(0, yext, 16, 2, yext, zf, zh)
     for copy in stress_halos[0:2]:
         copy.start()
     for i, comp in enumerate(YCOMP):
@@ -448,7 +448,47 @@
         await_all(3, j, r4, ROWS)
         for c in range(3):
             spectrum = jnp.transpose(r4[j, :, c].reshape(2 * MC * ROWS, 256))
-            fluid[c] += product(split(spectrum, INV), [ti[p, j] for p in range(INV)])
+            out = product(split(spectrum, INV), [ti[p, j] for p in range(INV)])
+            fluid[c] += out.reshape(16, 16, NX)
+
+    def tile_copies():
+        peers = ((row, col_peer(1)), (row, col_peer(COLS - 1)), (row_peer(1), col), (row_peer(ROWS - 1), col))
+        return [
+            remote(gtile.at[2], nbtile.at[k], halo_send.at[8 + k], halo_recv.at[8 + k], peer)
+            for k, peer in enumerate(peers)
+        ]
+
+    def neighbours():
+        for copy in tile_copies():
+            copy.wait_recv()
+        for k in range(4):
+            tile = nbtile[k]
+            nbcol[k] = dot_exact((pair == runs_lane).astype(F32), tile, NT)
+            ids = dot_exact(spread_runs[0:32], tile, NT)[:, 5:6] * 0.25
+            for r in range(ROWS):
+                match[r, 32 + 32 * k : 64 + 32 * k] = (ids == g2[r, 0:1]).astype(F32)
+            line, block = tile[3:4], tile[4:5]
+            y = jnp.floor(line * (1.0 / 16.0))
+            z = line - 16.0 * y
+            layer, along = (z, y) if k < 2 else (y, z)
+            layer = layer - (14.0 if k % 2 == 0 else 0.0)
+            inside = (layer >= 0.0) & (layer <= 1.0)
+            target = jnp.where(inside, block * 32.0 + layer * 16.0 + along, -1.0)
+            hits = (target == pair.astype(F32)).astype(F32)
+            nbhot[k] = hits.astype(BF16)
+            nbkeep[k] = jnp.broadcast_to(1.0 - jnp.sum(hits, axis=1, keepdims=True), (128, 128))
+
+    def rigid_of(sums, cols):
+        sums = dot_exact(gather_runs[:, 0:32], sums)
+        rx, ry, rz, mean, turn = (cols[:, k : k + 1] for k in (0, 1, 2, 6, 7))
+        vx, vy, vz = (sums[:, k : k + 1] * mean for k in range(3))
+        wx, wy, wz = (sums[:, k : k + 1] * turn for k in range(3, 6))
+        cell_x = rx + (lane128.astype(F32) - 63.5)
+        return (
+            jnp.broadcast_to(vx + wy * rz - wz * ry, (128, 128)),
+            vy + wz * cell_x - wx * rz,
+            vz + wx * ry - wy * cell_x,
+        )
 
     def geometry():
         wait_for(g2.at[pl.ds(0, ROWS - 1)], g_recv.at[1])
@@ -459,7 +499,7 @@
         for r in range(ROWS):
             block = g2[r]
             same = (ids == block[0:1]).astype(F32)
-            match[r] = same
+            match[r, 0:32] = same
             count += jnp.sum(same, axis=1, keepdims=True)
             cx += jnp.sum(same * block[1:2], axis=1, keepdims=True)
             cy += jnp.sum(same * block[2:3], axis=1, keepdims=True)
@@ -471,18 +511,23 @@
             block = g2[r]
             dx, dy, dz = block[1:2] - cx, block[2:3] - cy, block[3:4] - cz
             inner_spread = block[4:5] + 512.0 * (dx * dx + dy * dy + dz * dz)
-            spread += jnp.sum(match[r] * inner_spread, axis=1, keepdims=True)
+            spread += jnp.sum(match[r, 0:32] * inner_spread, axis=1, keepdims=True)
         inertia = jnp.maximum(spread * (2.0 / 3.0), 1.0)
         place = lane128
         packed = jnp.where(place == 0, 1.0 / jnp.maximum(512.0 * count, 1.0), 0.0)
         for at, value in ((1, cx), (2, cy), (3, cz), (4, 1.0 / inertia)):
             packed = jnp.where(place == at, value, packed)
-        geo[...] = packed
         mine = dot_exact((pair == runs_lane).astype(F32), fields, NT)
         centers = dot_exact(gather_runs[:, 0:32], packed)
         rel = jnp.where(place == 0, mine[:, 1:2] + 63.5 - centers[:, 1:2], 0.0)
         rel = jnp.where(place == 1, mine[:, 2:3] - centers[:, 2:3], rel)
-        mgeo[...] = jnp.where(place == 2, mine[:, 3:4] - centers[:, 3:4], rel)
+        rel = jnp.where(place == 2, mine[:, 3:4] - centers[:, 3:4], rel)
+        for at, value in enumerate((mine[:, 6:7], mine[:, 7:8], mine[:, 0:1], centers[:, 0:1], centers[:, 4:5])):
+            rel = jnp.where(place == 3 + at, value, rel)
+        mgeo[...] = rel
+        gtile[2] = jnp.transpose(rel)[0:8]
+        for copy in tile_copies():
+            copy.start()
         rows256 = lax.broadcasted_iota(jnp.int32, (256, 128), 0).astype(F32)
         cols256 = lax.broadcasted_iota(jnp.int32, (128, 256), 1).astype(F32)
         for b in range(4):
@@ -499,9 +544,19 @@
     def _(t):
         pl.when(t < CHUNKS)(lambda: y_forward(t))
         pl.when(t + 2 < CHUNKS)(lambda: x_forward(t + 2))
+        pl.when(t == 3)(neighbours)
         pl.when((t >= 2) & (t < CHUNKS + 2))(lambda: solve(t - 2))
         pl.when((t >= 4) & (t < CHUNKS + 4))(lambda: y_inverse(t - 4))
         pl.when(t >= 5)(lambda: x_inverse(t - 5))
+
+    for copy in stress_halos:
+        copy.wait_send()
+    for c in range(3):
+        for layer, z in enumerate((0, 1, 14, 15)):
+            zf[c, layer] = fluid[c, :, z, :]
+    velocity_halos = halo_copies(4, fluid, 14, 0, vext, zf, vzh)
+    for copy in velocity_halos:
+        copy.start()
 
     inside = lane128.astype(F32) - 63.5
     blocks = []
@@ -509,7 +564,7 @@
     for c in range(3):
         block = jnp.zeros((128, 128), F32)
         for b in range(4):
-            block += exact_left(hott[b], fluid[c, :, 128 * b : 128 * b + 128], 3)
+            block += exact_left(hott[b], fluid[c, :, :, 128 * b : 128 * b + 128].reshape(256, 128), 3)
         blocks.append(block)
         firsts.append(jnp.sum(block, axis=1, keepdims=True))
         seconds.append(jnp.sum(block * inside, axis=1, keepdims=True))
@@ -530,41 +585,32 @@
     gather_cols(1, g3)
     gather_rows(1, g3, g4)
     wait_for(g4.at[pl.ds(0, ROWS - 1)], g_recv.at[3])
-    totals = jnp.zeros((32, 8), F32)
+    totals = jnp.zeros((160, 8), F32)
     for r in range(ROWS):
         totals += dot_exact(match[r], g4[r], NT)
-    packed = geo[...]
-    params = jnp.zeros((32, 128), F32)
-    for at in range(6):
-        scale = packed[:, 0:1] if at < 3 else packed[:, 4:5]
-        params = jnp.where(lane128 == at, totals[:, at : at + 1] * scale, params)
-    fitted = dot_exact(gather_runs[:, 0:32], params)
-    vx, vy, vz, wx, wy, wz = (fitted[:, k : k + 1] for k in range(6))
-    cell_x = rx + inside
-    rigid = (
-        vx + wy * rz - wz * ry,
-        vy + wz * cell_x - wx * rz,
-        vz + wx * ry - wy * cell_x,
-    )
+    rigid = rigid_of(totals[0:32], mgeo)
     for c in range(3):
         fix = rigid[c] - blocks[c]
         for b in range(4):
             lanes = slice(128 * b, 128 * b + 128)
-            done = fluid[c, :, lanes] + exact_left(hot[b], fix, 3)
-            vext[c, 2:18, :, lanes] = done.reshape(16, 16, 128)
-    for copy in stress_halos:
-        copy.wait_send()
-    for c in range(3):
-        for layer, z in enumerate((0, 1, 14, 15)):
-            zf[c, layer] = vext[c, 2:18, z, :]
-    velocity_halos = halo_copies(4, vext, zf, vzh)
-    for copy in velocity_halos:
-        copy.start()
+            done = fluid[c, :, :, lanes] + exact_left(hot[b], fix, 3).reshape(16, 16, 128)
+            vext[c, 2:18, :, lanes] = done
     stores = [pltpu.make_async_copy(vext.at[c, 2:18], vext_out.at[c, 2:18], store_sem.at[c]) for c in range(3)]
     for store in stores:
         store.start()
     for copy in velocity_halos:
         copy.wait_recv()
+    for k in range(4):
+        rigid = rigid_of(totals[32 + 32 * k : 64 + 32 * k], nbcol[k])
+        fix = exact_left(nbhot[k], jnp.concatenate(rigid, axis=1), 3)
+        keep = nbkeep[k]
+        ref, first = ((vzh, 0), (vzh, 2), (vext, 0), (vext, 18))[k]
+        for c in range(3):
+            for b in range(4):
+                lanes, rows = slice(128 * b, 128 * b + 128), slice(32 * b, 32 * b + 32)
+                old = ref[c, first : first + 2, :, lanes].reshape(32, 128)
+                new = old * keep[rows] + fix[rows, 128 * c : 128 * c + 128]
+                ref[c, first : first + 2, :, lanes] = new.reshape(2, 16, 128)
     late = [
         pltpu.make_async_copy(vext.at[:, 0:2], vext_out.at[:, 0:2], store_sem.at[3]),
         pltpu.make_async_copy(vext.at[:, 18:20], vext_out.at[:, 18:20], store_sem.at[4]),
@@ -574,7 +620,7 @@
         store.start()
     stores += late
 
-    for copy in velocity_halos:
+    for copy in velocity_halos + tile_copies():
         copy.wait_send()
     wait_for(g1.at[pl.ds(0, COLS - 1)], g_send.at[0])
     wait_for(g2.at[pl.ds(0, ROWS - 1)], g_send.at[1])
@@ -640,7 +686,7 @@
         pltpu.VMEM((3, 4, 16, NX), F32),
         pltpu.VMEM((3, 256, NX), F32),
         pltpu.VMEM((2, 3, 256, NX), BF16),
-        pltpu.VMEM((3, 256, NX), F32),
+        pltpu.VMEM((3, 16, 16, NX), F32),
         pltpu.VMEM((CHUNKS, ROWS, 3, 2 * MC, 256), F32),
         pltpu.VMEM((CHUNKS, ROWS, 3, 2 * MC, 256), F32),
         pltpu.VMEM((CHUNKS, COLS, 3, 2, MC, 128), F32),
@@ -655,14 +701,17 @@
         pltpu.VMEM((ROWS, 8, 512), F32),
         pltpu.VMEM((COLS, 8, 128), F32),
         pltpu.VMEM((ROWS, 8, 512), F32),
-        pltpu.VMEM((2, 8, 128), F32),
-        pltpu.VMEM((ROWS, 32, 512), F32),
-        pltpu.VMEM((32, 128), F32),
+        pltpu.VMEM((3, 8, 128), F32),
+        pltpu.VMEM((ROWS, 160, 512), F32),
         pltpu.VMEM((128, 128), F32),
         pltpu.VMEM((4, 256, 128), BF16),
         pltpu.VMEM((4, 128, 256), BF16),
-        sems((8,)),
-        sems((8,)),
+        pltpu.VMEM((4, 8, 128), F32),
+        pltpu.VMEM((4, 128, 8), F32),
+        pltpu.VMEM((4, 128, 128), BF16),
+        pltpu.VMEM((4, 128, 128), F32),
+        sems((12,)),
+        sems((12,)),
         sems((4, CHUNKS)),
         sems((4, CHUNKS)),
         sems((4,)),

time: 105 us -> 106 us (level)
  Pallas kernels: 104 us -> 106 us
    pallas_call x1, Pallas kernels: 96.2 us -> 97.3 us  [local(): pl.pallas_call(kernel, out_shape=(jax.ShapeDtypeStruct((3, 20, 16, NX), F...]
where the time goes in v4:
time: 106 us
  Pallas kernels  106 us (100%)
    pallas_call x1, Pallas kernels, local(): pl.pallas_call(kernel, out_shape=(jax.ShapeDtypeStruct((3, 20, 16, NX), F...  97.3 us
    pallas_call x1, Pallas kernels, local(): pl.pallas_call(functools.partial(update, lines=lines), grid=(16 // lines,...  8.23 us

profile of v4, /device:TPU:1, one launch (start us, length us, event | category | flops | bytes accessed | tf_op | source)
XLA Modules:
  0.0 106.2 jit_solution(5907262142171677577)
XLA Ops:
  0.6 97.3 %shard_map.184 = (f32[3,20,16,512]{3,2,1,0:T(8,128)}, f32[3,4,16,512]{3,2,1,0:T(8,128)}) custom-call(f32[3,16,16,512]{3,2,1,0:T(8,128)} %force_in.1, f32[6,16,16,512]{3,2,1,0:T(8,128)} %mult.1, f32[6,16,16,512]{3,2,1,0:T(8,128)} %aux_in.1, s32[1,128]{1,0:T(1,128)} %bitcast.5, s32[1,128]{1,0:T(1,128)} %bitcast.6, s32[1,128]{1,0:T(1,128)} %bitcast.7, ...), custom_call_target="tpu_custom_call" | custom-call | tf_op jit(solution)/shard_map/pallas_call | solution.py:722
  97.9 8.2 %shard_map.185 = (f32[3,16,16,512]{3,2,1,0:T(8,128)}, f32[6,16,16,512]{3,2,1,0:T(8,128)}, f32[6,16,16,512]{3,2,1,0:T(8,128)}) custom-call(f32[3,20,16,512]{3,2,1,0:T(8,128)} %get-tuple-element.5.vlow.vhigh, f32[3,20,16,512]{3,2,1,0:T(8,128)} %get-tuple-element.5.vlow.vhigh, f32[3,64,512]{2,1,0:T(8,128)} %bitcast.4, f32[6,16,16,512]{3,2,1,0:T(8,128)} %mult.1, ...), custom_call_target="tpu_custom_call" | custom-call | tf_op jit(solution)/shard_map/pallas_call | solution.py:748

commit v5 on v4

--- a/solution.py
+++ b/solution.py
@@ -466,7 +466,8 @@
             nbcol[k] = dot_exact((pair == runs_lane).astype(F32), tile, NT)
             ids = dot_exact(spread_runs[0:32], tile, NT)[:, 5:6] * 0.25
             for r in range(ROWS):
-                match[r, 32 + 32 * k : 64 + 32 * k] = (ids == g2[r, 0:1]).astype(F32)
+                same = (ids == g2[r, 0:1]).astype(F32)
+                match[32 + 32 * k : 64 + 32 * k, 512 * r : 512 * r + 512] = same.astype(BF16)
             line, block = tile[3:4], tile[4:5]
             y = jnp.floor(line * (1.0 / 16.0))
             z = line - 16.0 * y
@@ -496,10 +497,12 @@
         ids = own[:, 0:1]
         count = jnp.zeros((32, 1), F32)
         cx, cy, cz = count, count, count
+        sames = []
         for r in range(ROWS):
             block = g2[r]
             same = (ids == block[0:1]).astype(F32)
-            match[r, 0:32] = same
+            match[0:32, 512 * r : 512 * r + 512] = same.astype(BF16)
+            sames.append(same)
             count += jnp.sum(same, axis=1, keepdims=True)
             cx += jnp.sum(same * block[1:2], axis=1, keepdims=True)
             cy += jnp.sum(same * block[2:3], axis=1, keepdims=True)
@@ -511,7 +514,7 @@
             block = g2[r]
             dx, dy, dz = block[1:2] - cx, block[2:3] - cy, block[3:4] - cz
             inner_spread = block[4:5] + 512.0 * (dx * dx + dy * dy + dz * dz)
-            spread += jnp.sum(match[r, 0:32] * inner_spread, axis=1, keepdims=True)
+            spread += jnp.sum(sames[r] * inner_spread, axis=1, keepdims=True)
         inertia = jnp.maximum(spread * (2.0 / 3.0), 1.0)
         place = lane128
         packed = jnp.where(place == 0, 1.0 / jnp.maximum(512.0 * count, 1.0), 0.0)
@@ -585,9 +588,10 @@
     gather_cols(1, g3)
     gather_rows(1, g3, g4)
     wait_for(g4.at[pl.ds(0, ROWS - 1)], g_recv.at[3])
-    totals = jnp.zeros((160, 8), F32)
-    for r in range(ROWS):
-        totals += dot_exact(match[r], g4[r], NT)
+    parts = split(jnp.concatenate([g4[r] for r in range(ROWS)], axis=1), 3)
+    parts = jnp.concatenate([part.astype(F32) for part in parts], axis=0).astype(BF16)
+    totals = dot(match[...], parts, NT)
+    totals = totals[:, 16:24] + totals[:, 8:16] + totals[:, 0:8]
     rigid = rigid_of(totals[0:32], mgeo)
     for c in range(3):
         fix = rigid[c] - blocks[c]
@@ -702,7 +706,7 @@
         pltpu.VMEM((COLS, 8, 128), F32),
         pltpu.VMEM((ROWS, 8, 512), F32),
         pltpu.VMEM((3, 8, 128), F32),
-        pltpu.VMEM((ROWS, 160, 512), F32),
+        pltpu.VMEM((160, 512 * ROWS), BF16),
         pltpu.VMEM((128, 128), F32),
         pltpu.VMEM((4, 256, 128), BF16),
         pltpu.VMEM((4, 128, 256), BF16),

time: 106 us -> 103 us (0.972)
  Pallas kernels: 106 us -> 102 us
    pallas_call x1, Pallas kernels: 97.3 us -> 93.8 us  [local(): pl.pallas_call(kernel, out_shape=(jax.ShapeDtypeStruct((3, 20, 16, NX), F...]
where the time goes in v5:
time: 103 us
  Pallas kernels  102 us (99%)
    pallas_call x1, Pallas kernels, local(): pl.pallas_call(kernel, out_shape=(jax.ShapeDtypeStruct((3, 20, 16, NX), F...  93.8 us
    pallas_call x1, Pallas kernels, local(): pl.pallas_call(functools.partial(update, lines=lines), grid=(16 // lines,...  8.24 us

profile of v5, /device:TPU:1, one launch (start us, length us, event | category | flops | bytes accessed | tf_op | source)
XLA Modules:
  0.0 102.7 jit_solution(18118674762550023759)
XLA Ops:
  0.6 93.8 %shard_map.184 = (f32[3,20,16,512]{3,2,1,0:T(8,128)}, f32[3,4,16,512]{3,2,1,0:T(8,128)}) custom-call(f32[3,16,16,512]{3,2,1,0:T(8,128)} %force_in.1, f32[6,16,16,512]{3,2,1,0:T(8,128)} %mult.1, f32[6,16,16,512]{3,2,1,0:T(8,128)} %aux_in.1, s32[1,128]{1,0:T(1,128)} %bitcast.5, s32[1,128]{1,0:T(1,128)} %bitcast.6, s32[1,128]{1,0:T(1,128)} %bitcast.7, ...), custom_call_target="tpu_custom_call" | custom-call | tf_op jit(solution)/shard_map/pallas_call | solution.py:726
  94.5 8.2 %shard_map.185 = (f32[3,16,16,512]{3,2,1,0:T(8,128)}, f32[6,16,16,512]{3,2,1,0:T(8,128)}, f32[6,16,16,512]{3,2,1,0:T(8,128)}) custom-call(f32[3,20,16,512]{3,2,1,0:T(8,128)} %get-tuple-element.5.vlow.vhigh, f32[3,20,16,512]{3,2,1,0:T(8,128)} %get-tuple-element.5.vlow.vhigh, f32[3,64,512]{2,1,0:T(8,128)} %bitcast.4, f32[6,16,16,512]{3,2,1,0:T(8,128)} %mult.1, ...), custom_call_target="tpu_custom_call" | custom-call | tf_op jit(solution)/shard_map/pallas_call | solution.py:752

commit v6 on v5

--- a/solution.py
+++ b/solution.py
@@ -480,7 +480,6 @@
             nbkeep[k] = jnp.broadcast_to(1.0 - jnp.sum(hits, axis=1, keepdims=True), (128, 128))
 
     def rigid_of(sums, cols):
-        sums = dot_exact(gather_runs[:, 0:32], sums)
         rx, ry, rz, mean, turn = (cols[:, k : k + 1] for k in (0, 1, 2, 6, 7))
         vx, vy, vz = (sums[:, k : k + 1] * mean for k in range(3))
         wx, wy, wz = (sums[:, k : k + 1] * turn for k in range(3, 6))
@@ -547,9 +546,9 @@
     def _(t):
         pl.when(t < CHUNKS)(lambda: y_forward(t))
         pl.when(t + 2 < CHUNKS)(lambda: x_forward(t + 2))
-        pl.when(t == 3)(neighbours)
         pl.when((t >= 2) & (t < CHUNKS + 2))(lambda: solve(t - 2))
         pl.when((t >= 4) & (t < CHUNKS + 4))(lambda: y_inverse(t - 4))
+        pl.when(t == CHUNKS + 3)(neighbours)
         pl.when(t >= 5)(lambda: x_inverse(t - 5))
 
     for copy in stress_halos:
@@ -592,7 +591,9 @@
     parts = jnp.concatenate([part.astype(F32) for part in parts], axis=0).astype(BF16)
     totals = dot(match[...], parts, NT)
     totals = totals[:, 16:24] + totals[:, 8:16] + totals[:, 0:8]
-    rigid = rigid_of(totals[0:32], mgeo)
+    groups = jnp.concatenate([totals[32 * k : 32 * k + 32] for k in range(5)], axis=1)
+    sums = dot_exact(gather_runs[:, 0:32], groups)
+    rigid = rigid_of(sums[:, 0:8], mgeo)
     for c in range(3):
         fix = rigid[c] - blocks[c]
         for b in range(4):
@@ -605,7 +606,7 @@
     for copy in velocity_halos:
         copy.wait_recv()
     for k in range(4):
-        rigid = rigid_of(totals[32 + 32 * k : 64 + 32 * k], nbcol[k])
+        rigid = rigid_of(sums[:, 8 * k + 8 : 8 * k + 16], nbcol[k])
         fix = exact_left(nbhot[k], jnp.concatenate(rigid, axis=1), 3)
         keep = nbkeep[k]
         ref, first = ((vzh, 0), (vzh, 2), (vext, 0), (vext, 18))[k]

time: 103 us -> 103 us (level)
  no operation moved by 1% of the time
where the time goes in v6:
time: 103 us
  Pallas kernels  102 us (99%)
    pallas_call x1, Pallas kernels, local(): pl.pallas_call(kernel, out_shape=(jax.ShapeDtypeStruct((3, 20, 16, NX), F...  94.2 us
    pallas_call x1, Pallas kernels, local(): pl.pallas_call(functools.partial(update, lines=lines), grid=(16 // lines,...  8.23 us

profile of v6, /device:TPU:1, one launch (start us, length us, event | category | flops | bytes accessed | tf_op | source)
XLA Modules:
  0.0 103.1 jit_solution(9177830899307779538)
XLA Ops:
  0.6 94.2 %shard_map.184 = (f32[3,20,16,512]{3,2,1,0:T(8,128)}, f32[3,4,16,512]{3,2,1,0:T(8,128)}) custom-call(f32[3,16,16,512]{3,2,1,0:T(8,128)} %force_in.1, f32[6,16,16,512]{3,2,1,0:T(8,128)} %mult.1, f32[6,16,16,512]{3,2,1,0:T(8,128)} %aux_in.1, s32[1,128]{1,0:T(1,128)} %bitcast.5, s32[1,128]{1,0:T(1,128)} %bitcast.6, s32[1,128]{1,0:T(1,128)} %bitcast.7, ...), custom_call_target="tpu_custom_call" | custom-call | tf_op jit(solution)/shard_map/pallas_call | solution.py:727
  94.8 8.2 %shard_map.185 = (f32[3,16,16,512]{3,2,1,0:T(8,128)}, f32[6,16,16,512]{3,2,1,0:T(8,128)}, f32[6,16,16,512]{3,2,1,0:T(8,128)}) custom-call(f32[3,20,16,512]{3,2,1,0:T(8,128)} %get-tuple-element.5.vlow.vhigh, f32[3,20,16,512]{3,2,1,0:T(8,128)} %get-tuple-element.5.vlow.vhigh, f32[3,64,512]{2,1,0:T(8,128)} %bitcast.4, f32[6,16,16,512]{3,2,1,0:T(8,128)} %mult.1, ...), custom_call_target="tpu_custom_call" | custom-call | tf_op jit(solution)/shard_map/pallas_call | solution.py:753

commit v7 on v6

--- a/solution.py
+++ b/solution.py
@@ -304,10 +304,9 @@
 
     def gather_cols(slot, buf):
         buf[col] = gtile[slot]
-        for off in range(1, COLS):
-            remote(
-                gtile.at[slot], buf.at[col], g_send.at[2 * slot], g_recv.at[2 * slot], (row, col_peer(off))
-            ).start()
+        for dy, dz in FAR:
+            peer = 4 * lax.rem(col // 4 + dz, 4) + lax.rem(col % 4 + dy, 4)
+            remote(gtile.at[slot], buf.at[col], g_send.at[2 * slot], g_recv.at[2 * slot], (row, peer)).start()
 
     def gather_rows(slot, buf, wide):
         wait_for(buf.at[pl.ds(0, COLS - 1)], g_recv.at[2 * slot])

time: 103 us -> 103 us (level)
  no operation moved by 1% of the time
where the time goes in v7:
time: 103 us
  Pallas kernels  102 us (99%)
    pallas_call x1, Pallas kernels, local(): pl.pallas_call(kernel, out_shape=(jax.ShapeDtypeStruct((3, 20, 16, NX), F...  93.7 us
    pallas_call x1, Pallas kernels, local(): pl.pallas_call(functools.partial(update, lines=lines), grid=(16 // lines,...  8.23 us

profile of v7, /device:TPU:1, one launch (start us, length us, event | category | flops | bytes accessed | tf_op | source)
XLA Modules:
  0.0 102.5 jit_solution(11584242779231110979)
XLA Ops:
  0.6 93.7 %shard_map.184 = (f32[3,20,16,512]{3,2,1,0:T(8,128)}, f32[3,4,16,512]{3,2,1,0:T(8,128)}) custom-call(f32[3,16,16,512]{3,2,1,0:T(8,128)} %force_in.1, f32[6,16,16,512]{3,2,1,0:T(8,128)} %mult.1, f32[6,16,16,512]{3,2,1,0:T(8,128)} %aux_in.1, s32[1,128]{1,0:T(1,128)} %bitcast.5, s32[1,128]{1,0:T(1,128)} %bitcast.6, s32[1,128]{1,0:T(1,128)} %bitcast.7, ...), custom_call_target="tpu_custom_call" | custom-call | tf_op jit(solution)/shard_map/pallas_call | solution.py:726
  94.3 8.2 %shard_map.185 = (f32[3,16,16,512]{3,2,1,0:T(8,128)}, f32[6,16,16,512]{3,2,1,0:T(8,128)}, f32[6,16,16,512]{3,2,1,0:T(8,128)}) custom-call(f32[3,20,16,512]{3,2,1,0:T(8,128)} %get-tuple-element.5.vlow.vhigh, f32[3,20,16,512]{3,2,1,0:T(8,128)} %get-tuple-element.5.vlow.vhigh, f32[3,64,512]{2,1,0:T(8,128)} %bitcast.4, f32[6,16,16,512]{3,2,1,0:T(8,128)} %mult.1, ...), custom_call_target="tpu_custom_call" | custom-call | tf_op jit(solution)/shard_map/pallas_call | solution.py:752
